TPU v7x, 1024 devices: a whole 4x8x16 slice. The times are simulated.
1024 devices in a mesh: gx: 16 (over z), gy: 4 (over y_hi), gz: 16 (over x, y_lo, core).
Axes of the slice: x: 4, y: 8 (y_hi: 4, y_lo: 2; y = y_hi * 2 + y_lo), z: 16, core: 2. Of those that a mesh axis runs over, the one named last changes fastest.
Arguments:
- orbitals: float32 [2, 256, 64, 2048], P(None, 'gx', 'gy', 'gz'), may hold values from -6 to 6
- potential: float32 [256, 64, 2048], P('gx', 'gy', 'gz'), may hold values from -2 to 1
- projectors: float32 [16, 4, 16, 8, 4, 4, 4096], P('gx', 'gy', 'gz'), as said below
- coupling: float32 [16, 4, 16, 8, 4, 4, 4], P('gx', 'gy', 'gz'), as said below
- block_starts: int32 [16, 4, 16, 8, 4, 3], P('gx', 'gy', 'gz'), may hold values from 0 to 127, as said below
- owner_counts: int32 [16, 4, 16, 8], P('gx', 'gy', 'gz'), may hold values from 1 to 4, as said below
Outputs:
- applied: float32 [2, 256, 64, 2048], P(None, 'gx', 'gy', 'gz')
Inputs may be any that keep to these rules, and one draw needn't show every extreme that they name: `block_starts`: entry [q, o, s, d] is the start along dimension d, inside its owner box, of the block of slot s of the box q - o (periodically, o = (a, b, c) with c fastest); it is below 16, 16, 128 for d = 0, 1, 2, and all eight copies of an atom agree. `owner_counts`: entry [q, o] is the number of live slots of the box q - o (periodically, o ordered as in block_starts); the eight copies agree. `projectors`: the eight copies of an atom's values agree. `coupling`: the eight copies of an atom's matrix agree.
All inputs are finite; a program needn't handle non-finite values.
Results may differ from a plain program's by a relative error of at most 0.00005.
Values sent between devices are 32-bit elements; how exact they have to be, the bound alone decides.
No kernel may reach another device: no remote copies, remote signals or barrier semaphores. Data moves between devices by JAX's collectives and lax.ppermute only.
A program may use at most 64 MiB of HBM per device.

v0:
```python
import jax
import jax.numpy as jnp
import numpy as np
from jax import lax
from jax.sharding import PartitionSpec as P

PB = 16
NPROJ = 4
SLOTS = 4


COEFF = [
    -5369.0 / 1800.0,
    12.0 / 7.0,
    -15.0 / 56.0,
    10.0 / 189.0,
    -1.0 / 112.0,
    2.0 / 1925.0,
    -1.0 / 16632.0,
]
CORNERS = np.array([[a, b, c] for a in (0, 1) for b in (0, 1) for c in (0, 1)], np.int32)


def passed_along(block, axis, distance):
    devices = range(lax.axis_size(axis))
    route = [((i - distance) % len(devices), i) for i in devices]
    return lax.ppermute(block, axis, route)


def extended(block, sides, width):
    for axis, dim in sides:
        count = lax.axis_size(axis)
        forward = [(i, i + 1) for i in range(count - 1)]
        forward.append((count - 1, 0))
        backward = [(target, source) for source, target in forward]
        low = lax.ppermute(
            lax.slice_in_dim(block, block.shape[dim] - width, None, axis=dim), axis, forward
        )
        high = lax.ppermute(lax.slice_in_dim(block, 0, width, axis=dim), axis, backward)
        block = jnp.concatenate([low, block, high], axis=dim)
    return block


def stencil_terms(padded, dim, extent):
    total = 0.0
    for step in range(1, 7):
        upper = lax.slice_in_dim(padded, 6 + step, 6 + step + extent, axis=dim)
        lower = lax.slice_in_dim(padded, 6 - step, 6 - step + extent, axis=dim)
        total = total + COEFF[step] * (upper + lower)
    return total


def move_x(value, offset):
    return passed_along(value, "gx", offset)


def move_y(value, offset):
    return passed_along(value, "gy", offset)


def move_z(value, offset):
    return passed_along(value, "gz", offset)


def owner_weights(partial_value, matrices, live, bands):
    width = SLOTS * bands * NPROJ
    cube = partial_value.reshape(2, 2, 2, width)
    part_x = cube[0] + move_x(cube[1], -1)
    part_y = part_x[0] + move_y(part_x[1], -1)
    total = part_y[0] + move_z(part_y[1], -1)
    sums = total.reshape(SLOTS, bands, NPROJ)
    own = (
        jnp.einsum("sij,sbj->sbi", matrices[0], sums, precision=lax.Precision.HIGHEST)
        * live[0][:, None, None]
    )
    flat = own.reshape(width)
    fan_z = jnp.stack([flat, move_z(flat, 1)])
    fan_y = jnp.stack([fan_z, move_y(fan_z, 1)])
    fan_x = jnp.stack([fan_y, move_x(fan_y, 1)])
    return fan_x.reshape(8, SLOTS, bands, NPROJ)


def on_device(orbitals, potential, projectors, coupling, block_starts, owner_counts):
    bands, cx, cy, cz = orbitals.shape
    padded = extended(orbitals, (("gx", 1), ("gy", 2), ("gz", 3)), 6)
    along_x = padded[:, :, 6 : 6 + cy, 6 : 6 + cz]
    along_y = padded[:, 6 : 6 + cx, :, 6 : 6 + cz]
    along_z = padded[:, 6 : 6 + cx, 6 : 6 + cy, :]
    laplace = 3.0 * COEFF[0] * orbitals
    laplace = laplace + stencil_terms(along_x, 1, cx)
    laplace = laplace + stencil_terms(along_y, 2, cy)
    laplace = laplace + stencil_terms(along_z, 3, cz)
    extent = np.array([cx, cy, cz], np.int32)
    starts = block_starts.reshape(8, SLOTS, 3)
    local = (
        jnp.maximum(starts - jnp.asarray(CORNERS * extent)[:, None, :] + PB, 0)
        .reshape(-1, 3)
        .astype(jnp.int32)
    )
    filled = jnp.pad(orbitals, ((0, 0), (PB, PB), (PB, PB), (PB, PB)))
    zero_index = jnp.zeros((), jnp.int32)

    def take_block(corner):
        return lax.dynamic_slice(
            filled, (zero_index, corner[0], corner[1], corner[2]), (bands, PB, PB, PB)
        )

    blocks = jax.vmap(take_block)(local).reshape(8 * SLOTS, bands, PB**3)
    values = projectors.reshape(8 * SLOTS, NPROJ, PB**3)
    partial_value = jnp.einsum("kbc,kjc->kbj", blocks, values, precision=lax.Precision.HIGHEST)
    matrices = coupling.reshape(8, SLOTS, NPROJ, NPROJ)
    live = (jnp.arange(SLOTS, dtype=jnp.int32)[None, :] < owner_counts.reshape(8, 1)).astype(
        jnp.float32
    )
    weighted = owner_weights(partial_value, matrices, live, bands)
    weighted = weighted.reshape(8 * SLOTS, bands, NPROJ)
    contrib = jnp.einsum("kbj,kjc->kbc", weighted, values, precision=lax.Precision.HIGHEST)
    contrib = contrib.reshape(8 * SLOTS, bands, PB, PB, PB)

    def add_block(index, accum):
        corner = local[index]
        where = (zero_index, corner[0], corner[1], corner[2])
        current = lax.dynamic_slice(accum, where, (bands, PB, PB, PB))
        piece = lax.dynamic_index_in_dim(contrib, index, 0, keepdims=False)
        return lax.dynamic_update_slice(accum, current + piece, where)

    spread_back = lax.fori_loop(0, 8 * SLOTS, add_block, jnp.zeros_like(filled), unroll=8)
    nonlocal_part = spread_back[:, PB : PB + cx, PB : PB + cy, PB : PB + cz]
    return -0.5 * laplace + potential[None] * orbitals + nonlocal_part


def solution(mesh):
    in_specs = (
        P(None, "gx", "gy", "gz"),
        P("gx", "gy", "gz"),
        P("gx", "gy", "gz", None, None, None, None),
        P("gx", "gy", "gz", None, None, None, None),
        P("gx", "gy", "gz", None, None, None),
        P("gx", "gy", "gz", None),
    )
    out_specs = P(None, "gx", "gy", "gz")
    return jax.shard_map(
        on_device, mesh=mesh, in_specs=in_specs, out_specs=out_specs, check_vma=False
    )
```

profile of v0, /device:TPU:856, one launch (start us, length us, event | category | flops | bytes accessed | tf_op | source)
XLA Modules:
  0.0 831.0 jit_solution(2749978373998878643)
XLA Ops:
  1.9 3.9 pad.4
  5.7 144.0 %while.20 = (s32[]{:T(128)}, f32[2,48,48,160]{3,2,1,0:T(8,128)}, s32[32,4]{0,1:T(4,128)S(1)}, f32[32,2,16,16,16]{4,3,2,1,0:T(8,128)}, s32[]{:T(128)}) while((s32[]{:T(128)}, f32[2,48,48,160]{3,2,1,0:T(8,128)}, s32[32,4]{0,1:T(4,128)S(1)}, f32[32,2,16,16,16]{4,3,2,1,0:T(8,128)}, s32[]{:T(128)}) %tuple.122), condition=%wide.while_cond, body=%wide.while_body.sunk | while | flops 2 | bytes 526457 | solution.py:104
  15.3 3.8 bitcast_dynamic-update-slice_fusion.2
  33.2 3.9 bitcast_dynamic-update-slice_fusion.2
  37.7 3.9 bitcast_dynamic-update-slice_fusion.2
  42.2 3.9 bitcast_dynamic-update-slice_fusion.2
  46.7 3.9 bitcast_dynamic-update-slice_fusion.2
  55.7 3.9 bitcast_dynamic-update-slice_fusion.2
  60.3 3.8 bitcast_dynamic-update-slice_fusion.2
  64.8 3.9 bitcast_dynamic-update-slice_fusion.2
  73.8 3.8 bitcast_dynamic-update-slice_fusion.2
  82.8 3.8 bitcast_dynamic-update-slice_fusion.2
  87.3 3.8 bitcast_dynamic-update-slice_fusion.2
  96.2 3.9 bitcast_dynamic-update-slice_fusion.2
  100.7 3.9 bitcast_dynamic-update-slice_fusion.2
  105.2 3.9 bitcast_dynamic-update-slice_fusion.2
  109.8 3.9 bitcast_dynamic-update-slice_fusion.2
  114.3 3.9 bitcast_dynamic-update-slice_fusion.2
  118.8 3.9 bitcast_dynamic-update-slice_fusion.2
  123.3 3.8 bitcast_dynamic-update-slice_fusion.2
  132.3 3.8 bitcast_dynamic-update-slice_fusion.2
  136.8 3.9 bitcast_dynamic-update-slice_fusion.2
  141.4 3.9 bitcast_dynamic-update-slice_fusion.2
  145.9 3.9 bitcast_dynamic-update-slice_fusion.2
  149.7 7.5 copy.57
  161.0 8.6 %fusion.73 = f32[32,2,4]{2,1,0:T(2,128)S(1)} fusion(f32[32,2,4096]{2,1,0:T(2,128)S(1)} %copy.58, f32[32,4,4096]{2,1,0:T(4,128)S(1)} %bitcast.152), kind=kOutput, calls=%fused_computation.150 | convolution fusion | flops 12582912 | bytes 3146752 | tf_op jit(solution)/shard_map/kbc,kjc->kbj/dot_general | solution.py:110
  177.8 4.9 collective-permute-done.7
  191.1 4.0 collective-permute-start.10
  201.5 4.7 collective-permute-start.1
  209.0 4.1 collective-permute-done
  214.7 5.2 collective-permute-start.3
  222.7 5.2 fusion.74
  228.0 4.2 copy.59
  232.2 9.0 %copy.60 = f32[32,2,16,16,16]{4,3,2,1,0:T(8,128)} copy(f32[32,2,16,16,16]{0,4,3,2,1:T(8,128)} %bitcast.155) | data formatting | bytes 2097152
  241.1 4.4 copy.50
  245.5 4.4 copy.49
  249.9 5.3 copy.51
  255.3 6.9 pad_maximum_fusion
  272.2 538.2 %while.21 = (s32[]{:T(128)}, f32[2,48,48,160]{3,2,1,0:T(8,128)}, s32[32,3]{0,1:T(4,128)S(1)}, f32[32,2,16,16,16]{4,3,2,1,0:T(8,128)}, s32[]{:T(128)}, /*index=5*...) while((s32[]{:T(128)}, f32[2,48,48,160]{3,2,1,0:T(8,128)}, ...), condition=%wide.region_1.2_spmd.clone.clone, body=%wide.region_0.1_spmd.clone.clone.clone.sunk | while | flops 65642 | bytes 1312685 | solution.py:127
  280.8 11.5 %dynamic_update_slice.112 = f32[2,48,48,160]{3,2,1,0:T(8,128)} dynamic-update-slice(f32[2,48,48,160]{3,2,1,0:T(8,128)} %get-tuple-element.473, f32[2,16,16,16]{3,2,1,0:T(8,128)S(1)} %bitcast_add_fusion.17, s32[]{:T(128)} %constant.141.clone.1..sunk, s32[]{:T(128)S(6)} %select_n.507, s32[]{:T(128)S(6)} %select_n.508, s32[]{:T(128)S(6)} %select_n.509) | dynamic-update-slice | bytes 65540 | tf_op jit(solution)/shard_map/while/body/eval_jaxpr/dynamic_update_slice | solution.py:125
  299.1 10.8 %dynamic_update_slice.113 = f32[2,48,48,160]{3,2,1,0:T(8,128)} dynamic-update-slice(f32[2,48,48,160]{3,2,1,0:T(8,128)} %dynamic_update_slice.112, f32[2,16,16,16]{3,2,1,0:T(8,128)S(1)} %bitcast_add_fusion.18, s32[]{:T(128)} %constant.141.clone.1..sunk, s32[]{:T(128)S(6)} %select_n.510, s32[]{:T(128)S(6)} %select_n.511, s32[]{:T(128)S(6)} %select_n.512) | dynamic-update-slice | bytes 65540 | tf_op jit(solution)/shard_map/while/body/eval_jaxpr/dynamic_update_slice | solution.py:125
  318.6 11.4 %dynamic_update_slice.114 = f32[2,48,48,160]{3,2,1,0:T(8,128)} dynamic-update-slice(f32[2,48,48,160]{3,2,1,0:T(8,128)} %dynamic_update_slice.113, f32[2,16,16,16]{3,2,1,0:T(8,128)S(1)} %bitcast_add_fusion.19, s32[]{:T(128)} %constant.141.clone.1..sunk, s32[]{:T(128)S(6)} %select_n.513, s32[]{:T(128)S(6)} %select_n.514, s32[]{:T(128)S(6)} %select_n.515) | dynamic-update-slice | bytes 65540 | tf_op jit(solution)/shard_map/while/body/eval_jaxpr/dynamic_update_slice | solution.py:125
  336.9 10.8 %dynamic_update_slice.115 = f32[2,48,48,160]{3,2,1,0:T(8,128)} dynamic-update-slice(f32[2,48,48,160]{3,2,1,0:T(8,128)} %dynamic_update_slice.114, f32[2,16,16,16]{3,2,1,0:T(8,128)S(1)} %bitcast_add_fusion.20, s32[]{:T(128)} %constant.141.clone.1..sunk, s32[]{:T(128)S(6)} %select_n.516, s32[]{:T(128)S(6)} %select_n.517, s32[]{:T(128)S(6)} %select_n.518) | dynamic-update-slice | bytes 65540 | tf_op jit(solution)/shard_map/while/body/eval_jaxpr/dynamic_update_slice | solution.py:125
  366.6 11.4 %dynamic_update_slice.117 = f32[2,48,48,160]{3,2,1,0:T(8,128)} dynamic-update-slice(f32[2,48,48,160]{3,2,1,0:T(8,128)} %dynamic_update_slice.116, f32[2,16,16,16]{3,2,1,0:T(8,128)S(1)} %bitcast_add_fusion.22, s32[]{:T(128)} %constant.141.clone.1..sunk, s32[]{:T(128)S(6)} %select_n.522, s32[]{:T(128)S(6)} %select_n.523, s32[]{:T(128)S(6)} %select_n.524) | dynamic-update-slice | bytes 65540 | tf_op jit(solution)/shard_map/while/body/eval_jaxpr/dynamic_update_slice | solution.py:125
  385.6 11.4 %dynamic_update_slice.118 = f32[2,48,48,160]{3,2,1,0:T(8,128)} dynamic-update-slice(f32[2,48,48,160]{3,2,1,0:T(8,128)} %dynamic_update_slice.117, f32[2,16,16,16]{3,2,1,0:T(8,128)S(1)} %bitcast_add_fusion.23, s32[]{:T(128)} %constant.141.clone.1..sunk, s32[]{:T(128)S(6)} %select_n.525, s32[]{:T(128)S(6)} %select_n.526, s32[]{:T(128)S(6)} %select_n.527) | dynamic-update-slice | bytes 65540 | tf_op jit(solution)/shard_map/while/body/eval_jaxpr/dynamic_update_slice | solution.py:125
  404.1 11.5 %dynamic_update_slice.119 = f32[2,48,48,160]{3,2,1,0:T(8,128)} dynamic-update-slice(f32[2,48,48,160]{3,2,1,0:T(8,128)} %dynamic_update_slice.118, f32[2,16,16,16]{3,2,1,0:T(8,128)S(1)} %bitcast_add_fusion.24, s32[]{:T(128)} %constant.141.clone.1..sunk, s32[]{:T(128)S(6)} %select_n.528, s32[]{:T(128)S(6)} %select_n.529, s32[]{:T(128)S(6)} %select_n.530) | dynamic-update-slice | bytes 65540 | tf_op jit(solution)/shard_map/while/body/eval_jaxpr/dynamic_update_slice | solution.py:125
  424.1 11.5 %dynamic_update_slice.112 = f32[2,48,48,160]{3,2,1,0:T(8,128)} dynamic-update-slice(f32[2,48,48,160]{3,2,1,0:T(8,128)} %get-tuple-element.473, f32[2,16,16,16]{3,2,1,0:T(8,128)S(1)} %bitcast_add_fusion.17, s32[]{:T(128)} %constant.141.clone.1..sunk, s32[]{:T(128)S(6)} %select_n.507, s32[]{:T(128)S(6)} %select_n.508, s32[]{:T(128)S(6)} %select_n.509) | dynamic-update-slice | bytes 65540 | tf_op jit(solution)/shard_map/while/body/eval_jaxpr/dynamic_update_slice | solution.py:125
  442.7 11.5 %dynamic_update_slice.113 = f32[2,48,48,160]{3,2,1,0:T(8,128)} dynamic-update-slice(f32[2,48,48,160]{3,2,1,0:T(8,128)} %dynamic_update_slice.112, f32[2,16,16,16]{3,2,1,0:T(8,128)S(1)} %bitcast_add_fusion.18, s32[]{:T(128)} %constant.141.clone.1..sunk, s32[]{:T(128)S(6)} %select_n.510, s32[]{:T(128)S(6)} %select_n.511, s32[]{:T(128)S(6)} %select_n.512) | dynamic-update-slice | bytes 65540 | tf_op jit(solution)/shard_map/while/body/eval_jaxpr/dynamic_update_slice | solution.py:125
  462.8 11.5 %dynamic_update_slice.114 = f32[2,48,48,160]{3,2,1,0:T(8,128)} dynamic-update-slice(f32[2,48,48,160]{3,2,1,0:T(8,128)} %dynamic_update_slice.113, f32[2,16,16,16]{3,2,1,0:T(8,128)S(1)} %bitcast_add_fusion.19, s32[]{:T(128)} %constant.141.clone.1..sunk, s32[]{:T(128)S(6)} %select_n.513, s32[]{:T(128)S(6)} %select_n.514, s32[]{:T(128)S(6)} %select_n.515) | dynamic-update-slice | bytes 65540 | tf_op jit(solution)/shard_map/while/body/eval_jaxpr/dynamic_update_slice | solution.py:125
  481.3 11.5 %dynamic_update_slice.115 = f32[2,48,48,160]{3,2,1,0:T(8,128)} dynamic-update-slice(f32[2,48,48,160]{3,2,1,0:T(8,128)} %dynamic_update_slice.114, f32[2,16,16,16]{3,2,1,0:T(8,128)S(1)} %bitcast_add_fusion.20, s32[]{:T(128)} %constant.141.clone.1..sunk, s32[]{:T(128)S(6)} %select_n.516, s32[]{:T(128)S(6)} %select_n.517, s32[]{:T(128)S(6)} %select_n.518) | dynamic-update-slice | bytes 65540 | tf_op jit(solution)/shard_map/while/body/eval_jaxpr/dynamic_update_slice | solution.py:125
  501.3 11.5 %dynamic_update_slice.116 = f32[2,48,48,160]{3,2,1,0:T(8,128)} dynamic-update-slice(f32[2,48,48,160]{3,2,1,0:T(8,128)} %dynamic_update_slice.115, f32[2,16,16,16]{3,2,1,0:T(8,128)S(1)} %bitcast_add_fusion.21, s32[]{:T(128)} %constant.141.clone.1..sunk, s32[]{:T(128)S(6)} %select_n.519, s32[]{:T(128)S(6)} %select_n.520, s32[]{:T(128)S(6)} %select_n.521) | dynamic-update-slice | bytes 65540 | tf_op jit(solution)/shard_map/while/body/eval_jaxpr/dynamic_update_slice | solution.py:125
  541.5 11.5 %dynamic_update_slice.119 = f32[2,48,48,160]{3,2,1,0:T(8,128)} dynamic-update-slice(f32[2,48,48,160]{3,2,1,0:T(8,128)} %dynamic_update_slice.118, f32[2,16,16,16]{3,2,1,0:T(8,128)S(1)} %bitcast_add_fusion.24, s32[]{:T(128)} %constant.141.clone.1..sunk, s32[]{:T(128)S(6)} %select_n.528, s32[]{:T(128)S(6)} %select_n.529, s32[]{:T(128)S(6)} %select_n.530) | dynamic-update-slice | bytes 65540 | tf_op jit(solution)/shard_map/while/body/eval_jaxpr/dynamic_update_slice | solution.py:125
  561.5 11.4 %dynamic_update_slice.112 = f32[2,48,48,160]{3,2,1,0:T(8,128)} dynamic-update-slice(f32[2,48,48,160]{3,2,1,0:T(8,128)} %get-tuple-element.473, f32[2,16,16,16]{3,2,1,0:T(8,128)S(1)} %bitcast_add_fusion.17, s32[]{:T(128)} %constant.141.clone.1..sunk, s32[]{:T(128)S(6)} %select_n.507, s32[]{:T(128)S(6)} %select_n.508, s32[]{:T(128)S(6)} %select_n.509) | dynamic-update-slice | bytes 65540 | tf_op jit(solution)/shard_map/while/body/eval_jaxpr/dynamic_update_slice | solution.py:125
  580.0 11.4 %dynamic_update_slice.113 = f32[2,48,48,160]{3,2,1,0:T(8,128)} dynamic-update-slice(f32[2,48,48,160]{3,2,1,0:T(8,128)} %dynamic_update_slice.112, f32[2,16,16,16]{3,2,1,0:T(8,128)S(1)} %bitcast_add_fusion.18, s32[]{:T(128)} %constant.141.clone.1..sunk, s32[]{:T(128)S(6)} %select_n.510, s32[]{:T(128)S(6)} %select_n.511, s32[]{:T(128)S(6)} %select_n.512) | dynamic-update-slice | bytes 65540 | tf_op jit(solution)/shard_map/while/body/eval_jaxpr/dynamic_update_slice | solution.py:125
  600.1 11.4 %dynamic_update_slice.114 = f32[2,48,48,160]{3,2,1,0:T(8,128)} dynamic-update-slice(f32[2,48,48,160]{3,2,1,0:T(8,128)} %dynamic_update_slice.113, f32[2,16,16,16]{3,2,1,0:T(8,128)S(1)} %bitcast_add_fusion.19, s32[]{:T(128)} %constant.141.clone.1..sunk, s32[]{:T(128)S(6)} %select_n.513, s32[]{:T(128)S(6)} %select_n.514, s32[]{:T(128)S(6)} %select_n.515) | dynamic-update-slice | bytes 65540 | tf_op jit(solution)/shard_map/while/body/eval_jaxpr/dynamic_update_slice | solution.py:125
  618.4 10.8 %dynamic_update_slice.115 = f32[2,48,48,160]{3,2,1,0:T(8,128)} dynamic-update-slice(f32[2,48,48,160]{3,2,1,0:T(8,128)} %dynamic_update_slice.114, f32[2,16,16,16]{3,2,1,0:T(8,128)S(1)} %bitcast_add_fusion.20, s32[]{:T(128)} %constant.141.clone.1..sunk, s32[]{:T(128)S(6)} %select_n.516, s32[]{:T(128)S(6)} %select_n.517, s32[]{:T(128)S(6)} %select_n.518) | dynamic-update-slice | bytes 65540 | tf_op jit(solution)/shard_map/while/body/eval_jaxpr/dynamic_update_slice | solution.py:125
  659.1 11.4 %dynamic_update_slice.118 = f32[2,48,48,160]{3,2,1,0:T(8,128)} dynamic-update-slice(f32[2,48,48,160]{3,2,1,0:T(8,128)} %dynamic_update_slice.117, f32[2,16,16,16]{3,2,1,0:T(8,128)S(1)} %bitcast_add_fusion.23, s32[]{:T(128)} %constant.141.clone.1..sunk, s32[]{:T(128)S(6)} %select_n.525, s32[]{:T(128)S(6)} %select_n.526, s32[]{:T(128)S(6)} %select_n.527) | dynamic-update-slice | bytes 65540 | tf_op jit(solution)/shard_map/while/body/eval_jaxpr/dynamic_update_slice | solution.py:125
  689.6 11.5 %dynamic_update_slice.112 = f32[2,48,48,160]{3,2,1,0:T(8,128)} dynamic-update-slice(f32[2,48,48,160]{3,2,1,0:T(8,128)} %get-tuple-element.473, f32[2,16,16,16]{3,2,1,0:T(8,128)S(1)} %bitcast_add_fusion.17, s32[]{:T(128)} %constant.141.clone.1..sunk, s32[]{:T(128)S(6)} %select_n.507, s32[]{:T(128)S(6)} %select_n.508, s32[]{:T(128)S(6)} %select_n.509) | dynamic-update-slice | bytes 65540 | tf_op jit(solution)/shard_map/while/body/eval_jaxpr/dynamic_update_slice | solution.py:125
  708.1 11.5 %dynamic_update_slice.113 = f32[2,48,48,160]{3,2,1,0:T(8,128)} dynamic-update-slice(f32[2,48,48,160]{3,2,1,0:T(8,128)} %dynamic_update_slice.112, f32[2,16,16,16]{3,2,1,0:T(8,128)S(1)} %bitcast_add_fusion.18, s32[]{:T(128)} %constant.141.clone.1..sunk, s32[]{:T(128)S(6)} %select_n.510, s32[]{:T(128)S(6)} %select_n.511, s32[]{:T(128)S(6)} %select_n.512) | dynamic-update-slice | bytes 65540 | tf_op jit(solution)/shard_map/while/body/eval_jaxpr/dynamic_update_slice | solution.py:125
  728.2 11.5 %dynamic_update_slice.114 = f32[2,48,48,160]{3,2,1,0:T(8,128)} dynamic-update-slice(f32[2,48,48,160]{3,2,1,0:T(8,128)} %dynamic_update_slice.113, f32[2,16,16,16]{3,2,1,0:T(8,128)S(1)} %bitcast_add_fusion.19, s32[]{:T(128)} %constant.141.clone.1..sunk, s32[]{:T(128)S(6)} %select_n.513, s32[]{:T(128)S(6)} %select_n.514, s32[]{:T(128)S(6)} %select_n.515) | dynamic-update-slice | bytes 65540 | tf_op jit(solution)/shard_map/while/body/eval_jaxpr/dynamic_update_slice | solution.py:125
  746.7 11.5 %dynamic_update_slice.115 = f32[2,48,48,160]{3,2,1,0:T(8,128)} dynamic-update-slice(f32[2,48,48,160]{3,2,1,0:T(8,128)} %dynamic_update_slice.114, f32[2,16,16,16]{3,2,1,0:T(8,128)S(1)} %bitcast_add_fusion.20, s32[]{:T(128)} %constant.141.clone.1..sunk, s32[]{:T(128)S(6)} %select_n.516, s32[]{:T(128)S(6)} %select_n.517, s32[]{:T(128)S(6)} %select_n.518) | dynamic-update-slice | bytes 65540 | tf_op jit(solution)/shard_map/while/body/eval_jaxpr/dynamic_update_slice | solution.py:125
  766.6 11.5 %dynamic_update_slice.116 = f32[2,48,48,160]{3,2,1,0:T(8,128)} dynamic-update-slice(f32[2,48,48,160]{3,2,1,0:T(8,128)} %dynamic_update_slice.115, f32[2,16,16,16]{3,2,1,0:T(8,128)S(1)} %bitcast_add_fusion.21, s32[]{:T(128)} %constant.141.clone.1..sunk, s32[]{:T(128)S(6)} %select_n.519, s32[]{:T(128)S(6)} %select_n.520, s32[]{:T(128)S(6)} %select_n.521) | dynamic-update-slice | bytes 65540 | tf_op jit(solution)/shard_map/while/body/eval_jaxpr/dynamic_update_slice | solution.py:125
  810.5 4.4 copy.52
  823.0 7.9 fusion.9
  (210 shorter events, 206.9 us)
Async XLA Ops:
  0.0 161.0 %copy-start = (f32[1,1,1,8,4,4,4096]{6,5,4,3,2,1,0:T(4,128)S(1)}, f32[1,1,1,8,4,4,4096]{6,5,4,3,2,1,0:T(4,128)}, u32[]{:S(2)}) copy-start(f32[1,1,1,8,4,4,4096]{6,5,4,3,2,1,0:T(4,128)} %param.11) | copy-start | bytes 6291460
  157.3 15.0 %copy-start.6 = (s32[1,1,1,8]{3,2,1,0:T(1,128)S(1)}, s32[1,1,1,8]{3,2,1,0:T(1,128)}, u32[]{:S(2)}) copy-start(s32[1,1,1,8]{3,2,1,0:T(1,128)} %param.14) | copy-start | bytes 100
  157.3 27.4 %copy-start.5 = (f32[1,1,1,8,4,4,4]{3,6,5,4,2,1,0:T(4,128)S(1)}, f32[1,1,1,8,4,4,4]{3,6,5,4,2,1,0:T(4,128)}, u32[]{:S(2)}) copy-start(f32[1,1,1,8,4,4,4]{3,6,5,4,2,1,0:T(4,128)} %param.12) | copy-start | bytes 6148
  157.3 43.6 %copy-start.2 = (f32[2,16,16,128]{3,2,1,0:T(8,128)S(1)}, f32[2,16,16,128]{3,2,1,0:T(8,128)}, u32[]{:S(2)}) copy-start(f32[2,16,16,128]{3,2,1,0:T(8,128)} %param.9) | copy-start | bytes 786436
  169.6 5.5 collective-permute-start.6
  175.1 7.6 collective-permute-start.7
  182.7 3.2 collective-permute-start.8
  186.2 4.9 collective-permute-start.9
  191.1 6.4 collective-permute-start.10
  197.5 10.7 %collective-permute-start.11 = (f32[2,2,32]{2,1,0:T(2,128)S(1)}, f32[2,2,32]{2,1,0:T(2,128)S(1)}, u32[]{:S(2)}, u32[]{:S(2)}) collective-permute-start(f32[2,2,32]{2,1,0:T(2,128)S(1)} %get-tuple-element.308), channel_id=1, source_target_pairs={{960,0},{0,64},{64,128},{128,192},{192,256},{256,320},{320,384},{3... | collective-permute-start | bytes 1544 | tf_op jit(solution)/shard_map/ppermute | solution.py:27
  201.5 7.4 collective-permute-start.1
  206.2 6.8 collective-permute-start
  214.7 30.8 %collective-permute-start.3 = (f32[2,28,6,128]{3,1,2,0:T(8,128)}, f32[2,28,6,128]{3,1,2,0:T(8,128)S(1)}, u32[]{:S(2)}, u32[]{:S(2)}) collective-permute-start(f32[2,28,6,128]{3,1,2,0:T(8,128)} %copy.62), channel_id=1, source_target_pairs={{0,16},{16,32},{32,48},{48,0},{1,17},{17,33},{33,49},{49,1},{2,18}... | collective-permute-start | bytes 516104 | tf_op jit(solution)/shard_map/ppermute | solution.py:36
  220.7 29.3 %collective-permute-start.2 = (f32[2,28,6,128]{3,1,2,0:T(8,128)}, f32[2,28,6,128]{3,1,2,0:T(8,128)}, u32[]{:S(2)}, u32[]{:S(2)}) collective-permute-start(f32[2,28,6,128]{3,1,2,0:T(8,128)} %copy.61), channel_id=1, source_target_pairs={{16,0},{32,16},{48,32},{0,48},{17,1},{33,17},{49,33},{1,49},{18,2}... | collective-permute-start | bytes 516104 | tf_op jit(solution)/shard_map/ppermute | solution.py:39
  245.5 16.6 %copy-start.4 = (f32[2,28,6,128]{3,1,2,0:T(8,128)}, f32[2,28,6,128]{3,1,2,0:T(8,128)S(1)}, u32[]{:S(2)}) copy-start(f32[2,28,6,128]{3,1,2,0:T(8,128)S(1)} %collective-permute-done.3) | copy-start | bytes 516100
  262.2 1.9 copy-start.1
  264.9 553.4 %collective-permute-start.4 = (f32[2,28,28,6]{2,1,3,0:T(8,128)}, f32[2,28,28,6]{2,1,3,0:T(8,128)}, u32[]{:S(2)}, u32[]{:S(2)}) collective-permute-start(f32[2,28,28,6]{2,1,3,0:T(8,128)} %get-tuple-element.292), channel_id=1, source_target_pairs={{1,0},{2,1},{3,2},{4,3},{5,4},{6,5},{7,6},{8,7},{9,8},{10,9},{11,1... | collective-permute-start | bytes 112904 | tf_op jit(solution)/shard_map/ppermute | solution.py:39
  266.8 553.8 %collective-permute-start.5 = (f32[2,28,28,6]{2,1,3,0:T(8,128)}, f32[2,28,28,6]{2,1,3,0:T(8,128)}, u32[]{:S(2)}, u32[]{:S(2)}) collective-permute-start(f32[2,28,28,6]{2,1,3,0:T(8,128)} %get-tuple-element.293), channel_id=1, source_target_pairs={{0,1},{1,2},{2,3},{3,4},{4,5},{5,6},{6,7},{7,8},{8,9},{9,10},{10,1... | collective-permute-start | bytes 112904 | tf_op jit(solution)/shard_map/ppermute | solution.py:36
  810.5 12.5 %copy-start.3 = (f32[2,16,16,128]{3,2,1,0:T(8,128)S(1)}, f32[2,16,16,128]{3,2,1,0:T(8,128)}, u32[]{:S(2)}) copy-start(f32[2,16,16,128]{3,2,1,0:T(8,128)} %param.9) | copy-start | bytes 786436
where the time goes:
time: 839 us; the launch traced here: 831 us
  local copies, waits for them, and re-layouts  522 us (62%)
  loops' own time  183 us (22%)
  other arithmetic  58.5 us (7%)
  starting transfers between devices  36.6 us (4%)
  waiting for transfers between devices  16.4 us (2%)
  matrix products  13.9 us (2%)
    dynamic_update_slice x32, local copies, waits for them, and re-layouts, add_block(): return lax.dynamic_update_slice(accum, current + piece, where)  293 us
    another operation x1, loops' own time, on_device(): lax.fori_loop(0, 8 * SLOTS, add_block, jnp.zeros_like(filled), unroll=8)  183 us
    gather x96, local copies, waits for them, and re-layouts  144 us
    add x32, other arithmetic, add_block(): return lax.dynamic_update_slice(accum, current + piece, where)  43.6 us
    ppermute x6, starting transfers between devices, passed_along(): return lax.ppermute(block, axis, route)  18.1 us
  transfers between devices with their start and end apart: 12, of which 6 were waited for; matrix products, arithmetic and copies ran while one was open for 48% of the time, Pallas kernels for 0%

commit v1 on v0

v1 whole, which is shorter than its diff:
```python
import jax
import jax.numpy as jnp
from jax import lax
from jax.experimental import pallas as pl
from jax.experimental.pallas import tpu as pltpu
from jax.sharding import PartitionSpec as P

PB = 16
NPROJ = 4
SLOTS = 4
BANDS = 2
CX = 16
CY = 16
CZ = 128
RADIUS = 6
EDGE = BANDS * RADIUS * CX
MiB = 1 << 20

COEFF = [
    -5369.0 / 1800.0,
    12.0 / 7.0,
    -15.0 / 56.0,
    10.0 / 189.0,
    -1.0 / 112.0,
    2.0 / 1925.0,
    -1.0 / 16632.0,
]
HALF = [-0.5 * c for c in COEFF]
HI = lax.Precision.HIGHEST
F32 = jnp.float32

VM = pl.BlockSpec(memory_space=pltpu.VMEM)
SM = pl.BlockSpec(memory_space=pltpu.SMEM)


def params():
    return pltpu.CompilerParams(vmem_limit_bytes=24 * MiB)


def iota(shape, dim):
    return lax.broadcasted_iota(jnp.int32, shape, dim)


def contract(a, b, dims):
    return lax.dot_general(a, b, (dims, ((), ())), precision=HI, preferred_element_type=F32)


def place(starts, counts, k):
    o = k >> 2
    s = k & 3
    lx = starts[0, 0, 0, o, s, 0] - CX * (o >> 2)
    ly = starts[0, 0, 0, o, s, 1] - CY * ((o >> 1) & 1)
    lz = starts[0, 0, 0, o, s, 2] - CZ * (o & 1)
    live = (s < counts[0, 0, 0, o]) & (lx > -PB) & (ly > -PB) & (lz > -PB)
    return lx, ly, lz, live


def z_inside(lz):
    z = (iota((8, 128), 1) & 15) + lz
    return (z >= 0) & (z < CZ)


def line_of(y):
    return jnp.where((y >= 0) & (y < CY), y, CY)


def splat(row):
    return jnp.broadcast_to(row, (8, 128))


def gather_kernel(starts, counts, x, proj, up_x, dn_x, up_y, dn_y, zed, part, turned, sums, rows):
    flat = x.reshape(BANDS * CX * CY, 128)
    zero = jnp.zeros((16, 128), F32)
    for b in range(BANDS):
        for y in range(CY):
            turned[b, y, 0:16, :] = zero
            turned[b, y, 32:48, :] = zero
            for h in range(2):
                turned[b, y, 16 + 8 * h : 24 + 8 * h, :] = flat[
                    pl.ds(256 * b + 128 * h + y, 8, stride=16), :
                ]
        turned[b, CY, :, :] = jnp.zeros((48, 128), F32)
    rows[...] = jnp.zeros_like(rows)
    group = iota((8, 128), 1) >> 4

    def atom(k, _):
        lx, ly, lz, live = place(starts, counts, k)

        @pl.when(live)
        def _():
            inside = z_inside(lz)
            acc = [None] * 8
            for h in range(2):
                packed = {}
                for r in range(8):
                    turn = (16 * r - lz + 128) & 127
                    y = line_of(ly + 8 * h + r)
                    for b in range(BANDS):
                        for q in range(2):
                            v = turned[b, y, pl.ds(lx + 16 + 8 * q, 8), :]
                            v = pltpu.roll(v, turn, 1)
                            packed[b, q] = v if r == 0 else jnp.where(group == r, v, packed[b, q])
                for q in range(2):
                    cells = [jnp.where(inside, packed[b, q], 0.0) for b in range(BANDS)]
                    for j in range(NPROJ):
                        p = proj[k, pl.ds(64 * q + 4 * h + j, 8, stride=8), :]
                        for b in range(BANDS):
                            n = b * NPROJ + j
                            t = cells[b] * p
                            acc[n] = t if acc[n] is None else acc[n] + t
            for n in range(8):
                sums[8 * n : 8 * n + 8, :] = acc[n]
            total = sums[pl.ds(0, 8, stride=8), :]
            for n in range(1, 8):
                total = total + sums[pl.ds(n, 8, stride=8), :]
            rows[pl.ds(pl.multiple_of(k * 8, 8), 8), :] = total

        return 0

    lax.fori_loop(0, 8 * SLOTS, atom, 0)
    coef = contract(jnp.ones((8, 128), F32), rows[...], ((1,), (1,)))
    part[0:8, :] = coef[:, 0:128]
    part[8:16, :] = coef[:, 128:256]
    for b in range(BANDS):
        up_x[96 * b : 96 * b + 96, :] = x[b, 10:16].reshape(96, 128)
        dn_x[96 * b : 96 * b + 96, :] = x[b, 0:6].reshape(96, 128)
    up_x[192:200, :] = coef[:, 0:128]
    dn_x[192:200, :] = coef[:, 128:256]
    for b in range(BANDS):
        for i in range(CX):
            at = (b * CX + i) * RADIUS
            up_y[at : at + RADIUS, :] = x[b, i, 10:16, :]
            dn_y[at : at + RADIUS, :] = x[b, i, 0:6, :]
    row, lane = iota((16, 128), 0), iota((16, 128), 1)
    pick_up = (row < 6) & (lane == row + 122)
    pick_dn = (row >= 8) & (row < 14) & (lane == row - 8)
    pick = jnp.where(pick_up | pick_dn, 1.0, 0.0).astype(F32)
    flat = x[...].reshape(BANDS * CX * CY, 128)
    zed[...] = contract(pick, flat, ((1,), (1,)))


def local_kernel(x, pot, out):
    row, lane = iota((128, 128), 0), iota((128, 128), 1)
    far = jnp.abs(row - lane)
    band = jnp.where(far == 0, 3.0 * HALF[0], 0.0)
    for k in range(1, 7):
        band = jnp.where(far == k, HALF[k], band)
    flat = x[...].reshape(BANDS * CX * CY, 128)
    out[...] = contract(flat, band.astype(F32), ((1,), (0,))).reshape(BANDS, CX, CY, CZ)
    for b in range(BANDS):
        out[b] = out[b] + pot[...] * x[b]


def x_kernel(x, low, high, acc, out):
    for b in range(BANDS):

        def plane(i, b=b):
            if i < 0:
                at = 96 * b + 16 * (i + 6)
                return low[at : at + 16, :]
            if i >= CX:
                at = 96 * b + 16 * (i - CX)
                return high[at : at + 16, :]
            return x[b, i]

        for i in range(CX):
            total = acc[b, i]
            for k in range(1, 7):
                total = total + HALF[k] * (plane(i + k) + plane(i - k))
            out[b, i] = total


def y_kernel(x, low, high, acc, out, wide):
    for b in range(BANDS):
        for i in range(CX):
            at = (b * CX + i) * RADIUS
            wide[b, i, 2:8, :] = low[at : at + RADIUS, :]
            wide[b, i, 8:24, :] = x[b, i]
            wide[b, i, 24:30, :] = high[at : at + RADIUS, :]

    for b in range(BANDS):

        def line(i, _, b=b):
            total = acc[b, i]
            for k in range(1, 7):
                total = total + HALF[k] * (
                    wide[b, i, 8 + k : 24 + k, :] + wide[b, i, 8 - k : 24 - k, :]
                )
            out[b, i] = total
            return 0

        lax.fori_loop(0, CX, line, 0, unroll=4)


def spread_kernel(starts, counts, coupling, proj, sums, z_lo, z_hi, acc, out, turned, coef):
    eye = iota((128, 128), 0) == iota((128, 128), 1)
    ones = jnp.ones((128, 128), F32)
    for a in range(2):
        row = jnp.broadcast_to(sums[8 * a : 8 * a + 1, :], (128, 128))
        coef[128 * a : 128 * a + 128, :] = contract(jnp.where(eye, row, 0.0), ones, ((1,), (0,)))
    turned[...] = jnp.zeros_like(turned)
    group = iota((8, 128), 1) >> 4

    def atom(k, _):
        lx, ly, lz, live = place(starts, counts, k)

        @pl.when(live)
        def _():
            inside = z_inside(lz)
            own = coef[pl.ds(pl.multiple_of(k * 8, 8), 8), :]
            weight = []
            for b in range(BANDS):
                c = [splat(own[b * NPROJ + j : b * NPROJ + j + 1, :]) for j in range(NPROJ)]
                for i in range(NPROJ):
                    total = coupling[0, 0, 0, k >> 2, k & 3, i, 0] * c[0]
                    for j in range(1, NPROJ):
                        total = total + coupling[0, 0, 0, k >> 2, k & 3, i, j] * c[j]
                    weight.append(total)
            for h in range(2):
                packed = {}
                for q in range(2):
                    p = [
                        proj[k, pl.ds(64 * q + 4 * h + j, 8, stride=8), :] for j in range(NPROJ)
                    ]
                    for b in range(BANDS):
                        v = weight[b * NPROJ] * p[0]
                        for j in range(1, NPROJ):
                            v = v + weight[b * NPROJ + j] * p[j]
                        packed[b, q] = jnp.where(inside, v, 0.0)
                for r in range(8):
                    turn = (lz - 16 * r + 256) & 127
                    y = line_of(ly + 8 * h + r)
                    for b in range(BANDS):
                        for q in range(2):
                            v = jnp.where(group == r, packed[b, q], 0.0)
                            v = pltpu.roll(v, turn, 1)
                            at = pl.ds(lx + 16 + 8 * q, 8)
                            turned[b, y, at, :] = turned[b, y, at, :] + v

        return 0

    lax.fori_loop(0, 8 * SLOTS, atom, 0)
    edge = jnp.concatenate([z_lo[...], z_hi[...]], axis=0)
    row, lane = iota((16, 128), 0), iota((16, 128), 1)
    low = row < 8
    far = jnp.where(low, lane + 6 - row, 128 + (row - 8) - lane)
    real = (row & 7) < 6
    tail = jnp.zeros((16, 128), F32)
    for k in range(1, 7):
        tail = jnp.where(real & (far == k), HALF[k], tail)
    z_part = contract(edge, tail, ((0,), (0,))).reshape(BANDS, CX, CY, CZ)
    flat = turned.reshape(BANDS * (CY + 1) * 48, 128)
    for b in range(BANDS):
        for i in range(CX):
            for h in range(2):
                first = (b * (CY + 1) + 8 * h) * 48 + 16 + i
                at = slice(8 * h, 8 * h + 8)
                spread = flat[pl.ds(first, 8, stride=48), :]
                out[b, i, at, :] = acc[b, i, at, :] + z_part[b, i, at, :] + spread


def shape(*dims):
    return jax.ShapeDtypeStruct(dims, F32)


def shifted(value, axis, distance):
    n = lax.axis_size(axis)
    return lax.ppermute(value, axis, [(i, (i + distance) % n) for i in range(n)])


def on_device(orbitals, potential, projectors, coupling, block_starts, owner_counts):
    grid = shape(BANDS, CX, CY, CZ)
    projectors = projectors.reshape(8, SLOTS, NPROJ, 32, 128).transpose(0, 1, 3, 2, 4)
    projectors = projectors.reshape(8 * SLOTS, 32 * NPROJ, 128)
    up_x, dn_x, up_y, dn_y, zed, part = pl.pallas_call(
        gather_kernel,
        out_shape=[
            shape(EDGE + 8, 128),
            shape(EDGE + 8, 128),
            shape(EDGE, 128),
            shape(EDGE, 128),
            shape(16, 512),
            shape(16, 128),
        ],
        in_specs=[SM, SM, VM, VM],
        out_specs=[VM] * 6,
        scratch_shapes=[
            pltpu.VMEM((BANDS, CY + 1, 48, 128), F32),
            pltpu.VMEM((64, 128), F32),
            pltpu.VMEM((256, 128), F32),
        ],
        compiler_params=params(),
        name="gather",
    )(block_starts, owner_counts, orbitals, projectors)

    from_low = shifted(up_x, "gx", 1)
    from_high = shifted(dn_x, "gx", -1)
    acc = pl.pallas_call(
        local_kernel,
        out_shape=grid,
        in_specs=[VM] * 2,
        out_specs=VM,
        compiler_params=params(),
        name="local",
    )(orbitals, potential)
    x_low, x_high = from_low[:EDGE], from_high[:EDGE]
    sums = part + jnp.concatenate([from_high[EDGE:], from_low[EDGE:]], axis=0)

    from_low = shifted(jnp.concatenate([up_y, sums], axis=0), "gy", 1)
    from_high = shifted(jnp.concatenate([dn_y, sums], axis=0), "gy", -1)
    acc = pl.pallas_call(
        x_kernel,
        out_shape=grid,
        in_specs=[VM] * 4,
        out_specs=VM,
        compiler_params=params(),
        name="along_x",
    )(orbitals, x_low, x_high, acc)
    y_low, y_high = from_low[:EDGE], from_high[:EDGE]
    lane = iota((16, 128), 1)
    first = (lane & 64) == 0
    sums = sums + jnp.where(
        first, jnp.roll(from_high[EDGE:], -64, 1), jnp.roll(from_low[EDGE:], 64, 1)
    )

    flat = sums.reshape(2, 8, 128).transpose(1, 0, 2).reshape(8, 256)
    from_low = shifted(jnp.concatenate([zed[0:8], flat], axis=1), "gz", 1)
    from_high = shifted(jnp.concatenate([zed[8:16], flat], axis=1), "gz", -1)
    acc = pl.pallas_call(
        y_kernel,
        out_shape=grid,
        in_specs=[VM] * 4,
        out_specs=VM,
        scratch_shapes=[pltpu.VMEM((BANDS, CX, 32, 128), F32)],
        compiler_params=params(),
        name="along_y",
    )(orbitals, y_low, y_high, acc)
    lane = iota((8, 256), 1)
    first = (lane & 32) == 0
    flat = flat + jnp.where(
        first, jnp.roll(from_high[:, 512:], -32, 1), jnp.roll(from_low[:, 512:], 32, 1)
    )
    sums = flat.reshape(8, 2, 128).transpose(1, 0, 2).reshape(16, 128)
    return pl.pallas_call(
        spread_kernel,
        out_shape=grid,
        in_specs=[SM, SM, SM] + [VM] * 5,
        out_specs=VM,
        scratch_shapes=[
            pltpu.VMEM((BANDS, CY + 1, 48, 128), F32),
            pltpu.VMEM((256, 128), F32),
        ],
        compiler_params=params(),
        name="spread",
    )(
        block_starts,
        owner_counts,
        coupling,
        projectors,
        sums,
        from_low[:, :512],
        from_high[:, :512],
        acc,
    )


def solution(mesh):
    in_specs = (
        P(None, "gx", "gy", "gz"),
        P("gx", "gy", "gz"),
        P("gx", "gy", "gz", None, None, None, None),
        P("gx", "gy", "gz", None, None, None, None),
        P("gx", "gy", "gz", None, None, None),
        P("gx", "gy", "gz", None),
    )
    out_specs = P(None, "gx", "gy", "gz")
    return jax.shard_map(
        on_device, mesh=mesh, in_specs=in_specs, out_specs=out_specs, check_vma=False
    )
```

time: 839 us -> 61.9 us (0.07)
  the two profiles are of different devices: /device:TPU:856 before, /device:TPU:6 now
where the time goes in v1:
time: 61.9 us; the launch traced here: 61.5 us
  starting transfers between devices  32.4 us (52%)
  waiting for transfers between devices  12.1 us (20%)
  Pallas kernels  12 us (19%)
  local copies, waits for them, and re-layouts  4.52 us (7%)
    ppermute x6, starting transfers between devices, shifted(): lax.ppermute(value, axis, [(i, (i + distance) % n) for i in range(n)])  32.4 us
    ppermute x6, waiting for transfers between devices, shifted(): lax.ppermute(value, axis, [(i, (i + distance) % n) for i in range(n)])  12.1 us
    pallas_call x1, Pallas kernels, on_device(): pl.pallas_call(spread_kernel, out_shape=grid, in_specs=[SM, SM, SM] + [VM...  6.78 us
    pallas_call x1, Pallas kernels, on_device(): pl.pallas_call(gather_kernel, out_shape=[shape(EDGE + 8, 128), shape(EDGE...  4.46 us
    unnamed x18, local copies, waits for them, and re-layouts  4.18 us
  transfers between devices with their start and end apart: 6, of which 5 were waited for; matrix products, arithmetic and copies ran while one was open for 1% of the time, Pallas kernels for 1%

profile of v1, /device:TPU:6, one launch (start us, length us, event | category | flops | bytes accessed | tf_op | source)
XLA Modules:
  0.0 61.5 jit_solution(15767710013684171743)
XLA Ops:
  0.0 0.8 %copy.9.starts = s32[1,1,1,8,4,3]{5,4,3,2,1,0:T(4,128)S(1)} copy(s32[1,1,1,8,4,3]{3,4,5,2,1,0:T(4,128)} %param.10) | data formatting | bytes 768 | tf_op args[4]
  0.8 0.0 copy-start
  0.8 1.6 %copy-done = f32[1,1,1,8,4,4,4096]{6,5,4,3,2,1,0:T(4,128)S(1)} copy-done((f32[1,1,1,8,4,4,4096]{6,5,4,3,2,1,0:T(4,128)S(1)}, f32[1,1,1,8,4,4,4096]{6,5,4,3,2,1,0:T(4,128)}, u32[]{:S(2)}) %copy-start) | copy-done | bytes 2097176
  2.4 0.0 copy-start.2
  2.4 0.9 %copy-done.2 = f32[2,16,16,128]{3,2,1,0:T(8,128)S(1)} copy-done((f32[2,16,16,128]{3,2,1,0:T(8,128)S(1)}, f32[2,16,16,128]{3,2,1,0:T(8,128)}, u32[]{:S(2)}) %copy-start.2) | copy-done | bytes 262168
  3.3 0.0 copy-start.5
  3.3 0.7 %copy-done.5 = s32[1,1,1,8]{3,2,1,0:T(1,128)S(1)} copy-done((s32[1,1,1,8]{3,2,1,0:T(1,128)S(1)}, s32[1,1,1,8]{3,2,1,0:T(1,128)}, u32[]{:S(2)}) %copy-start.5) | copy-done | bytes 56
  4.0 0.0 copy-start.7
  4.0 0.0 copy-start.3
  4.0 0.0 copy-start.4
  4.0 4.5 %gather.1 = (f32[200,128]{1,0:T(8,128)S(1)}, f32[200,128]{1,0:T(8,128)S(1)}, f32[192,128]{1,0:T(8,128)S(1)}, f32[192,128]{1,0:T(8,128)S(1)}, f32[16,512]{1,0:T(8,128)S(1)}, /*index=5*/f32[16,128]{1,0:T(8,128)S(1)}) custom-call(s32[1,1,1,8,4,3]{5,4,3,2,1,0:T(4,128)S(1)} %copy.9.starts, s32[1,1,1,8]{3,2,1,0:T(1,128)S(1)} %copy-done.5, ...), custom_call_target="tpu_custom_call" | custom-call | tf_op jit(solution)/shard_map/gather/pallas_call | solution.py:275
  8.5 3.7 %collective-permute-start.1 = (f32[200,128]{1,0:T(8,128)S(1)}, f32[200,128]{1,0:T(8,128)S(1)}, u32[]{:S(2)}, u32[]{:S(2)}) collective-permute-start(f32[200,128]{1,0:T(8,128)S(1)} %get-tuple-element.13), channel_id=1, source_target_pairs={{0,64},{64,128},{128,192},{192,256},{256,320},{320,384},{384,448},... | collective-permute-start | bytes 307208 | tf_op jit(solution)/shard_map/ppermute | solution.py:268
  12.2 15.7 %collective-permute-start = (f32[200,128]{1,0:T(8,128)S(1)}, f32[200,128]{1,0:T(8,128)S(1)}, u32[]{:S(2)}, u32[]{:S(2)}) collective-permute-start(f32[200,128]{1,0:T(8,128)S(1)} %get-tuple-element.12), channel_id=1, source_target_pairs={{0,960},{64,0},{128,64},{192,128},{256,192},{320,256},{384,320},{4... | collective-permute-start | bytes 307208 | tf_op jit(solution)/shard_map/ppermute | solution.py:268
  27.9 0.7 %collective-permute-done.1 = f32[200,128]{1,0:T(8,128)S(1)} collective-permute-done((f32[200,128]{1,0:T(8,128)S(1)}, f32[200,128]{1,0:T(8,128)S(1)}, u32[]{:S(2)}, u32[]{:S(2)}) %collective-permute-start.1) | collective-permute-done | bytes 102432 | tf_op jit(solution)/shard_map/ppermute | solution.py:268
  28.6 1.5 %collective-permute-done = f32[200,128]{1,0:T(8,128)S(1)} collective-permute-done((f32[200,128]{1,0:T(8,128)S(1)}, f32[200,128]{1,0:T(8,128)S(1)}, u32[]{:S(2)}, u32[]{:S(2)}) %collective-permute-start) | collective-permute-done | bytes 102432 | tf_op jit(solution)/shard_map/ppermute | solution.py:268
  30.1 0.0 copy-start.1
  30.1 0.0 copy-start.6
  30.2 6.7 %collective-permute-start.2 = (f32[208,128]{1,0:T(8,128)S(1)}, f32[208,128]{1,0:T(8,128)S(1)}, u32[]{:S(2)}, u32[]{:S(2)}) collective-permute-start(f32[208,128]{1,0:T(8,128)S(1)} %get-tuple-element.26), channel_id=1, source_target_pairs={{0,48},{16,0},{32,16},{48,32},{1,49},{17,1},{33,17},{49,33},{2,50}... | collective-permute-start | bytes 319496 | tf_op jit(solution)/shard_map/ppermute | solution.py:268
  36.9 1.9 %collective-permute-start.3 = (f32[208,128]{1,0:T(8,128)S(1)}, f32[208,128]{1,0:T(8,128)S(1)}, u32[]{:S(2)}, u32[]{:S(2)}) collective-permute-start(f32[208,128]{1,0:T(8,128)S(1)} %get-tuple-element.25), channel_id=1, source_target_pairs={{0,16},{16,32},{32,48},{48,0},{1,17},{17,33},{33,49},{49,1},{2,18}... | collective-permute-start | bytes 319496 | tf_op jit(solution)/shard_map/ppermute | solution.py:268
  38.9 1.4 %collective-permute-done.2 = f32[208,128]{1,0:T(8,128)S(1)} collective-permute-done((f32[208,128]{1,0:T(8,128)S(1)}, f32[208,128]{1,0:T(8,128)S(1)}, u32[]{:S(2)}, u32[]{:S(2)}) %collective-permute-start.2) | collective-permute-done | bytes 106528 | tf_op jit(solution)/shard_map/ppermute | solution.py:268
  40.2 0.1 fusion.5
  40.3 6.1 %collective-permute-done.3 = f32[208,128]{1,0:T(8,128)S(1)} collective-permute-done((f32[208,128]{1,0:T(8,128)S(1)}, f32[208,128]{1,0:T(8,128)S(1)}, u32[]{:S(2)}, u32[]{:S(2)}) %collective-permute-start.3) | collective-permute-done | bytes 106528 | tf_op jit(solution)/shard_map/ppermute | solution.py:268
  46.4 0.1 fusion.4
  46.5 0.1 fusion
  46.6 1.9 %collective-permute-start.4 = (f32[8,768]{1,0:T(8,128)S(1)}, f32[8,768]{1,0:T(8,128)S(1)}, u32[]{:S(2)}, u32[]{:S(2)}) collective-permute-start(f32[8,768]{1,0:T(8,128)S(1)} %get-tuple-element.24), channel_id=1, source_target_pairs={{0,15},{1,0},{2,1},{3,2},{4,3},{5,4},{6,5},{7,6},{8,7},{9,8},{10,9... | collective-permute-start | bytes 73736 | tf_op jit(solution)/shard_map/ppermute | solution.py:268
  48.5 2.4 %collective-permute-start.5 = (f32[8,768]{1,0:T(8,128)S(1)}, f32[8,768]{1,0:T(8,128)S(1)}, u32[]{:S(2)}, u32[]{:S(2)}) collective-permute-start(f32[8,768]{1,0:T(8,128)S(1)} %get-tuple-element.23), channel_id=1, source_target_pairs={{0,1},{1,2},{2,3},{3,4},{4,5},{5,6},{6,7},{7,8},{8,9},{9,10},{10,1... | collective-permute-start | bytes 73736 | tf_op jit(solution)/shard_map/ppermute | solution.py:268
  50.9 0.0 copy-done.7
  50.9 0.2 copy.10.coupling
  51.1 0.0 copy-done.3
  51.1 0.0 copy-done.4
  51.1 0.4 local.1.acc
  51.5 0.2 along_x.1.acc
  51.7 0.3 along_y.1.acc
  52.0 0.0 collective-permute-done.4
  52.0 0.1 slice.98
  52.1 2.4 %collective-permute-done.5 = f32[8,768]{1,0:T(8,128)S(1)} collective-permute-done((f32[8,768]{1,0:T(8,128)S(1)}, f32[8,768]{1,0:T(8,128)S(1)}, u32[]{:S(2)}, u32[]{:S(2)}) %collective-permute-start.5) | collective-permute-done | bytes 24608 | tf_op jit(solution)/shard_map/ppermute | solution.py:268
  54.5 0.1 slice.100
  54.6 0.1 fusion.3.sums
  54.7 0.0 copy-done.1
  54.7 0.0 copy-done.6
  54.7 6.8 %spread.1 = f32[2,16,16,128]{3,2,1,0:T(8,128)} custom-call(s32[1,1,1,8,4,3]{5,4,3,2,1,0:T(4,128)S(1)} %copy.9.starts, s32[1,1,1,8]{3,2,1,0:T(1,128)S(1)} %copy-done.6, f32[1,1,1,8,4,4,4]{6,5,4,3,2,1,0:T(4,128)S(1)} %copy.10.coupling, f32[32,128,128]{2,1,0:T(8,128)S(1)} %bitcast.28, f32[16,128]{1,0:T(8,128)S(1)} %fusion.3.sums, f32[8,512]{1,0:T(8,128)S(1)} %slice.102.z_lo, ...), custom_call_target="tpu_custom_call" | custom-call | tf_op jit(solution)/shard_map/spread/pallas_call | solution.py:344
  (16 shorter events, 0.1 us)
Async XLA Ops:
  0.8 1.6 %copy-start = (f32[1,1,1,8,4,4,4096]{6,5,4,3,2,1,0:T(4,128)S(1)}, f32[1,1,1,8,4,4,4096]{6,5,4,3,2,1,0:T(4,128)}, u32[]{:S(2)}) copy-start(f32[1,1,1,8,4,4,4096]{6,5,4,3,2,1,0:T(4,128)} %param.8) | copy-start | bytes 6291460
  2.4 0.9 %copy-start.2 = (f32[2,16,16,128]{3,2,1,0:T(8,128)S(1)}, f32[2,16,16,128]{3,2,1,0:T(8,128)}, u32[]{:S(2)}) copy-start(f32[2,16,16,128]{3,2,1,0:T(8,128)} %x.7) | copy-start | bytes 786436
  3.3 0.7 %copy-start.5 = (s32[1,1,1,8]{3,2,1,0:T(1,128)S(1)}, s32[1,1,1,8]{3,2,1,0:T(1,128)}, u32[]{:S(2)}) copy-start(s32[1,1,1,8]{3,2,1,0:T(1,128)} %counts.3) | copy-start | bytes 100
  4.0 46.9 %copy-start.7 = (f32[1,1,1,8,4,4,4]{3,6,5,4,2,1,0:T(4,128)S(1)}, f32[1,1,1,8,4,4,4]{3,6,5,4,2,1,0:T(4,128)}, u32[]{:S(2)}) copy-start(f32[1,1,1,8,4,4,4]{3,6,5,4,2,1,0:T(4,128)} %param.9) | copy-start | bytes 6148
  4.0 47.1 %copy-start.3 = (f32[2,16,16,128]{3,2,1,0:T(8,128)S(1)}, f32[2,16,16,128]{3,2,1,0:T(8,128)}, u32[]{:S(2)}) copy-start(f32[2,16,16,128]{3,2,1,0:T(8,128)} %x.7) | copy-start | bytes 786436
  4.0 47.1 %copy-start.4 = (f32[16,16,128]{2,1,0:T(8,128)S(1)}, f32[16,16,128]{2,1,0:T(8,128)}, u32[]{:S(2)}) copy-start(f32[16,16,128]{2,1,0:T(8,128)} %pot.1) | copy-start | bytes 393220
  8.5 20.1 %collective-permute-start.1 = (f32[200,128]{1,0:T(8,128)S(1)}, f32[200,128]{1,0:T(8,128)S(1)}, u32[]{:S(2)}, u32[]{:S(2)}) collective-permute-start(f32[200,128]{1,0:T(8,128)S(1)} %get-tuple-element.13), channel_id=1, source_target_pairs={{0,64},{64,128},{128,192},{192,256},{256,320},{320,384},{384,448},... | collective-permute-start | bytes 307208 | tf_op jit(solution)/shard_map/ppermute | solution.py:268
  12.2 18.0 %collective-permute-start = (f32[200,128]{1,0:T(8,128)S(1)}, f32[200,128]{1,0:T(8,128)S(1)}, u32[]{:S(2)}, u32[]{:S(2)}) collective-permute-start(f32[200,128]{1,0:T(8,128)S(1)} %get-tuple-element.12), channel_id=1, source_target_pairs={{0,960},{64,0},{128,64},{192,128},{256,192},{320,256},{384,320},{4... | collective-permute-start | bytes 307208 | tf_op jit(solution)/shard_map/ppermute | solution.py:268
  30.1 24.5 %copy-start.1 = (f32[1,1,1,8,4,4,4096]{6,5,4,3,2,1,0:T(4,128)S(1)}, f32[1,1,1,8,4,4,4096]{6,5,4,3,2,1,0:T(4,128)}, u32[]{:S(2)}) copy-start(f32[1,1,1,8,4,4,4096]{6,5,4,3,2,1,0:T(4,128)} %param.8) | copy-start | bytes 6291460
  30.1 24.5 %copy-start.6 = (s32[1,1,1,8]{3,2,1,0:T(1,128)S(1)}, s32[1,1,1,8]{3,2,1,0:T(1,128)}, u32[]{:S(2)}) copy-start(s32[1,1,1,8]{3,2,1,0:T(1,128)} %counts.3) | copy-start | bytes 100
  30.2 10.1 %collective-permute-start.2 = (f32[208,128]{1,0:T(8,128)S(1)}, f32[208,128]{1,0:T(8,128)S(1)}, u32[]{:S(2)}, u32[]{:S(2)}) collective-permute-start(f32[208,128]{1,0:T(8,128)S(1)} %get-tuple-element.26), channel_id=1, source_target_pairs={{0,48},{16,0},{32,16},{48,32},{1,49},{17,1},{33,17},{49,33},{2,50}... | collective-permute-start | bytes 319496 | tf_op jit(solution)/shard_map/ppermute | solution.py:268
  36.9 9.5 %collective-permute-start.3 = (f32[208,128]{1,0:T(8,128)S(1)}, f32[208,128]{1,0:T(8,128)S(1)}, u32[]{:S(2)}, u32[]{:S(2)}) collective-permute-start(f32[208,128]{1,0:T(8,128)S(1)} %get-tuple-element.25), channel_id=1, source_target_pairs={{0,16},{16,32},{32,48},{48,0},{1,17},{17,33},{33,49},{49,1},{2,18}... | collective-permute-start | bytes 319496 | tf_op jit(solution)/shard_map/ppermute | solution.py:268
  46.6 5.4 %collective-permute-start.4 = (f32[8,768]{1,0:T(8,128)S(1)}, f32[8,768]{1,0:T(8,128)S(1)}, u32[]{:S(2)}, u32[]{:S(2)}) collective-permute-start(f32[8,768]{1,0:T(8,128)S(1)} %get-tuple-element.24), channel_id=1, source_target_pairs={{0,15},{1,0},{2,1},{3,2},{4,3},{5,4},{6,5},{7,6},{8,7},{9,8},{10,9... | collective-permute-start | bytes 73736 | tf_op jit(solution)/shard_map/ppermute | solution.py:268
  48.5 6.0 %collective-permute-start.5 = (f32[8,768]{1,0:T(8,128)S(1)}, f32[8,768]{1,0:T(8,128)S(1)}, u32[]{:S(2)}, u32[]{:S(2)}) collective-permute-start(f32[8,768]{1,0:T(8,128)S(1)} %get-tuple-element.23), channel_id=1, source_target_pairs={{0,1},{1,2},{2,3},{3,4},{4,5},{5,6},{6,7},{7,8},{8,9},{9,10},{10,1... | collective-permute-start | bytes 73736 | tf_op jit(solution)/shard_map/ppermute | solution.py:268

commit v2 on v1

v2 whole, which is shorter than its diff:
```python
import jax
import jax.numpy as jnp
from jax import lax
from jax.experimental import pallas as pl
from jax.experimental.pallas import tpu as pltpu
from jax.sharding import PartitionSpec as P

PB = 16
NPROJ = 4
SLOTS = 4
BANDS = 2
CX = 16
CY = 16
CZ = 128
RADIUS = 6
EDGE = BANDS * RADIUS * CX
MiB = 1 << 20

COEFF = [
    -5369.0 / 1800.0,
    12.0 / 7.0,
    -15.0 / 56.0,
    10.0 / 189.0,
    -1.0 / 112.0,
    2.0 / 1925.0,
    -1.0 / 16632.0,
]
HALF = [-0.5 * c for c in COEFF]
HI = lax.Precision.HIGHEST
F32 = jnp.float32

VM = pl.BlockSpec(memory_space=pltpu.VMEM)
HB = pl.BlockSpec(memory_space=pl.ANY)
PLACES = [
    pltpu.SMEM((1, 1, 1, 3, SLOTS, 8), jnp.int32),
    pltpu.SMEM((1, 1, 1, 8), jnp.int32),
]
MATRICES = [pltpu.SMEM((1, 1, 1, SLOTS, NPROJ, NPROJ, 8), F32)]
LISTED = [pltpu.SMEM((8 * SLOTS,), jnp.int32), pltpu.SemaphoreType.DMA((3,))]


def params():
    return pltpu.CompilerParams(vmem_limit_bytes=24 * MiB)


def iota(shape, dim):
    return lax.broadcasted_iota(jnp.int32, shape, dim)


def contract(a, b, dims):
    return lax.dot_general(a, b, (dims, ((), ())), precision=HI, preferred_element_type=F32)


def place(starts, counts, k):
    o = k >> 2
    s = k & 3
    lx = starts[0, 0, 0, 0, s, o] - CX * (o >> 2)
    ly = starts[0, 0, 0, 1, s, o] - CY * ((o >> 1) & 1)
    lz = starts[0, 0, 0, 2, s, o] - CZ * (o & 1)
    live = (s < counts[0, 0, 0, o]) & (lx > -PB) & (ly > -PB) & (lz > -PB)
    whole = (lz >= 0) & (lz <= CZ - PB)
    return lx, ly, lz, live, whole


def begin(pairs, sems):
    copies = [pltpu.make_async_copy(a, b, sems.at[n]) for n, (a, b) in enumerate(pairs)]
    for copy in copies:
        copy.start()
    return copies


def chosen(starts, counts, which, listed):
    n = jnp.int32(0)
    for k in range(8 * SLOTS):
        _, _, _, live, whole = place(starts, counts, k)
        listed[n] = k
        n = n + which(live, whole).astype(jnp.int32)
    return n


def line_of(y):
    return jnp.where((y >= 0) & (y < CY), y, CY)


def splat(row):
    return jnp.broadcast_to(row, (8, 128))


def turn_about(source, target):
    flat = source.reshape(BANDS * CX * CY, 128)
    zero = jnp.zeros((16, 128), F32)
    for b in range(BANDS):
        for y in range(CY):
            target[b, y, 0:16, :] = zero
            target[b, y, 32:48, :] = zero
            for h in range(2):
                target[b, y, 16 + 8 * h : 24 + 8 * h, :] = flat[
                    pl.ds(256 * b + 128 * h + y, 8, stride=16), :
                ]
        target[b, CY, :, :] = jnp.zeros((48, 128), F32)


def turn_kernel(x, same, turned, up_x, dn_x, up_y, dn_y):
    same[...] = x[...]
    turn_about(x, turned)
    for b in range(BANDS):
        up_x[96 * b : 96 * b + 96, :] = x[b, 10:16].reshape(96, 128)
        dn_x[96 * b : 96 * b + 96, :] = x[b, 0:6].reshape(96, 128)
        for i in range(CX):
            at = (b * CX + i) * RADIUS
            up_y[at : at + RADIUS, :] = x[b, i, 10:16, :]
            dn_y[at : at + RADIUS, :] = x[b, i, 0:6, :]


def gather_kernel(
    starts_in, counts_in, turned, proj, part, sums, rows, starts, counts, listed, sems
):
    copies = begin([(starts_in, starts), (counts_in, counts)], sems)
    rows[...] = jnp.zeros_like(rows)
    for copy in copies:
        copy.wait()
    group = iota((8, 128), 1) >> 4
    cell = iota((8, 128), 1) & 15

    def atom(n, _):
        k = listed[n]
        lx, ly, lz, _, _ = place(starts, counts, k)
        inside = (cell + lz >= 0) & (cell + lz < CZ)
        acc = [None] * 8
        for h in range(2):
            packed = {}
            for r in range(8):
                turn = (16 * r - lz + 128) & 127
                y = line_of(ly + 8 * h + r)
                for b in range(BANDS):
                    for q in range(2):
                        v = turned[b, y, pl.ds(lx + 16 + 8 * q, 8), :]
                        v = pltpu.roll(v, turn, 1)
                        packed[b, q] = v if r == 0 else jnp.where(group == r, v, packed[b, q])
            for q in range(2):
                cells = [jnp.where(inside, packed[b, q], 0.0) for b in range(BANDS)]
                for j in range(NPROJ):
                    p = proj[k, pl.ds(64 * q + 4 * h + j, 8, stride=8), :]
                    for b in range(BANDS):
                        m = b * NPROJ + j
                        t = cells[b] * p
                        acc[m] = t if acc[m] is None else acc[m] + t
        for m in range(8):
            sums[8 * m : 8 * m + 8, :] = acc[m]
        total = sums[pl.ds(0, 8, stride=8), :]
        for m in range(1, 8):
            total = total + sums[pl.ds(m, 8, stride=8), :]
        rows[pl.ds(pl.multiple_of(k * 8, 8), 8), :] = total

        return 0

    number = chosen(starts, counts, lambda live, whole: live, listed)
    lax.fori_loop(0, number, atom, 0)
    coef = contract(jnp.ones((8, 128), F32), rows[...], ((1,), (1,)))
    part[0:8, :] = coef[:, 0:128]
    part[8:16, :] = coef[:, 128:256]


def local_kernel(x, pot, out, up_z, dn_z):
    row, lane = iota((128, 128), 0), iota((128, 128), 1)
    near = jnp.abs(row - lane)
    band = jnp.where(near == 0, 3.0 * HALF[0], 0.0)
    for k in range(1, 7):
        band = jnp.where(near == k, HALF[k], band)
    flat = x[...].reshape(BANDS * CX * CY, 128)
    total = contract(flat, band.astype(F32), ((1,), (0,)))
    out[...] = total.reshape(BANDS, CX, CY, CZ)
    for b in range(BANDS):
        out[b] = out[b] + pot[...] * x[b]
    row, lane = iota((16, 128), 0), iota((16, 128), 1)
    pick_up = (row < 6) & (lane == row + 122)
    pick_dn = (row >= 8) & (row < 14) & (lane == row - 8)
    pick = jnp.where(pick_up | pick_dn, 1.0, 0.0).astype(F32)
    faces = contract(pick, flat, ((1,), (1,)))
    up_z[...] = faces[0:8]
    dn_z[...] = faces[8:16]


def x_kernel(x, low, high, acc, out):
    for b in range(BANDS):

        def plane(i, b=b):
            if i < 0:
                at = 96 * b + 16 * (i + 6)
                return low[at : at + 16, :]
            if i >= CX:
                at = 96 * b + 16 * (i - CX)
                return high[at : at + 16, :]
            return x[b, i]

        for i in range(CX):
            total = acc[b, i]
            for k in range(1, 7):
                total = total + HALF[k] * (plane(i + k) + plane(i - k))
            out[b, i] = total


def y_kernel(x, low, high, acc, out, wide):
    for b in range(BANDS):
        for i in range(CX):
            at = (b * CX + i) * RADIUS
            wide[b, i, 2:8, :] = low[at : at + RADIUS, :]
            wide[b, i, 8:24, :] = x[b, i]
            wide[b, i, 24:30, :] = high[at : at + RADIUS, :]

    for b in range(BANDS):

        def line(i, _, b=b):
            total = acc[b, i]
            for k in range(1, 7):
                total = total + HALF[k] * (
                    wide[b, i, 8 + k : 24 + k, :] + wide[b, i, 8 - k : 24 - k, :]
                )
            out[b, i] = total
            return 0

        lax.fori_loop(0, CX, line, 0, unroll=4)


def spread(cut, copies, tables, listed, proj, sums, turned, coef):
    starts, counts, coupling = tables
    eye = iota((128, 128), 0) == iota((128, 128), 1)
    ones = jnp.ones((128, 128), F32)
    for a in range(2):
        row = jnp.broadcast_to(sums[8 * a : 8 * a + 1, :], (128, 128))
        coef[128 * a : 128 * a + 128, :] = contract(jnp.where(eye, row, 0.0), ones, ((1,), (0,)))
    turned[...] = jnp.zeros_like(turned)
    group = iota((8, 128), 1) >> 4
    cell = iota((8, 128), 1) & 15

    for copy in copies:
        copy.wait()

    def atom(n, _):
        k = listed[n]
        lx, ly, lz, _, _ = place(starts, counts, k)
        inside = (cell + lz >= 0) & (cell + lz < CZ)
        own = coef[pl.ds(pl.multiple_of(k * 8, 8), 8), :]
        weight = []
        for b in range(BANDS):
            c = [splat(own[b * NPROJ + j : b * NPROJ + j + 1, :]) for j in range(NPROJ)]
            for i in range(NPROJ):
                total = coupling[0, 0, 0, k & 3, i, 0, k >> 2] * c[0]
                for j in range(1, NPROJ):
                    total = total + coupling[0, 0, 0, k & 3, i, j, k >> 2] * c[j]
                weight.append(total)
        for h in range(2):
            packed = {}
            for q in range(2):
                p = [
                    proj[k, pl.ds(64 * q + 4 * h + j, 8, stride=8), :] for j in range(NPROJ)
                ]
                for b in range(BANDS):
                    v = weight[b * NPROJ] * p[0]
                    for j in range(1, NPROJ):
                        v = v + weight[b * NPROJ + j] * p[j]
                    packed[b, q] = jnp.where(inside, v, 0.0)
            for half in range(2):
                batch = []
                for r in range(4 * half, 4 * half + 4):
                    turn = (lz - 16 * r + 256) & 127
                    y = line_of(ly + 8 * h + r)
                    for b in range(BANDS):
                        for q in range(2):
                            v = jnp.where(group == r, packed[b, q], 0.0)
                            at = pl.ds(lx + 16 + 8 * q, 8)
                            v = turned[b, y, at, :] + pltpu.roll(v, turn, 1)
                            batch.append((b, y, at, v))
                for b, y, at, v in batch:
                    turned[b, y, at, :] = v

        return 0

    if cut:
        number = chosen(starts, counts, lambda live, whole: live & jnp.logical_not(whole), listed)
    else:
        number = chosen(starts, counts, lambda live, whole: live & whole, listed)
    lax.fori_loop(0, number, atom, 0)


def fold(b, i, h, turned):
    flat = turned.reshape(BANDS * (CY + 1) * 48, 128)
    return flat[pl.ds((b * (CY + 1) + 8 * h) * 48 + 16 + i, 8, stride=48), :]


def whole_kernel(
    starts_in, counts_in, coupling_in, proj, sums, acc, out, turned, coef,
    starts, counts, coupling, listed, sems,
):
    tables = (starts, counts, coupling)
    copies = begin(list(zip((starts_in, counts_in, coupling_in), tables)), sems)
    spread(False, copies, tables, listed, proj, sums, turned, coef)
    for b in range(BANDS):
        for i in range(CX):
            for h in range(2):
                at = slice(8 * h, 8 * h + 8)
                out[b, i, at, :] = acc[b, i, at, :] + fold(b, i, h, turned)


def cut_kernel(
    starts_in, counts_in, coupling_in, proj, sums, z_low, z_high, acc, out, turned, coef,
    starts, counts, coupling, listed, sems,
):
    tables = (starts, counts, coupling)
    copies = begin(list(zip((starts_in, counts_in, coupling_in), tables)), sems)
    edge = jnp.concatenate([z_low[...], z_high[...]], axis=0)
    row, lane = iota((16, 128), 0), iota((16, 128), 1)
    far = jnp.where(row < 8, lane + 6 - row, 128 + (row - 8) - lane)
    real = (row & 7) < 6
    tail = jnp.zeros((16, 128), F32)
    for k in range(1, 7):
        tail = jnp.where(real & (far == k), HALF[k], tail)
    z_part = contract(edge, tail, ((0,), (0,))).reshape(BANDS, CX, CY, CZ)
    out[...] = acc[...] + z_part
    spread(True, copies, tables, listed, proj, sums, turned, coef)
    for b in range(BANDS):
        for i in range(CX):
            for h in range(2):
                at = slice(8 * h, 8 * h + 8)
                out[b, i, at, :] = out[b, i, at, :] + fold(b, i, h, turned)


def shape(*dims):
    return jax.ShapeDtypeStruct(dims, F32)


def shifted(value, axis, distance):
    n = lax.axis_size(axis)
    return lax.ppermute(value, axis, [(i, (i + distance) % n) for i in range(n)])


def call(kernel, outs, ins, scratch, name, args, flops, bytes_accessed):
    return pl.pallas_call(
        kernel,
        out_shape=outs,
        in_specs=ins,
        out_specs=[VM] * len(outs),
        scratch_shapes=[pltpu.VMEM(s, F32) if isinstance(s, tuple) else s for s in scratch],
        compiler_params=params(),
        cost_estimate=pl.CostEstimate(
            flops=flops, bytes_accessed=bytes_accessed, transcendentals=0
        ),
        name=name,
    )(*args)


def on_device(orbitals, potential, projectors, coupling, block_starts, owner_counts):
    grid = shape(BANDS, CX, CY, CZ)
    padded = (BANDS, CY + 1, 48, 128)
    projectors = projectors.reshape(8, SLOTS, NPROJ, 32, 128).transpose(0, 1, 3, 2, 4)
    projectors = projectors.reshape(8 * SLOTS, 32 * NPROJ, 128)
    starts = block_starts.transpose(0, 1, 2, 5, 4, 3)
    matrices = coupling.transpose(0, 1, 2, 4, 5, 6, 3)

    same, turned, up_x, dn_x, up_y, dn_y = call(
        turn_kernel,
        [grid, shape(*padded)] + [shape(EDGE, 128)] * 4,
        [VM],
        [],
        "turn",
        (orbitals,),
        1 << 30,
        1 << 24,
    )
    (part,) = call(
        gather_kernel,
        [shape(16, 128)],
        [HB, HB, VM, VM],
        [(64, 128), (256, 128)] + PLACES + LISTED,
        "gather",
        (starts, owner_counts, turned, projectors),
        1 << 30,
        1 << 24,
    )

    from_low = shifted(jnp.concatenate([up_x, part[:8]], axis=0), "gx", 1)
    from_high = shifted(jnp.concatenate([dn_x, part[8:]], axis=0), "gx", -1)
    acc, up_z, dn_z = call(
        local_kernel,
        [grid, shape(8, 512), shape(8, 512)],
        [VM] * 2,
        [],
        "local",
        (same, potential),
        1 << 26,
        1 << 20,
    )
    part, acc = lax.optimization_barrier((part, acc))
    x_low, x_high = from_low[:EDGE], from_high[:EDGE]
    sums = part + jnp.concatenate([from_high[EDGE:], from_low[EDGE:]], axis=0)

    from_low = shifted(jnp.concatenate([up_y, sums], axis=0), "gy", 1)
    from_high = shifted(jnp.concatenate([dn_y, sums], axis=0), "gy", -1)
    (acc,) = call(
        x_kernel, [grid], [VM] * 4, [], "along_x", (same, x_low, x_high, acc), 1 << 22, 1 << 20
    )
    sums, acc = lax.optimization_barrier((sums, acc))
    y_low, y_high = from_low[:EDGE], from_high[:EDGE]
    first = (iota((16, 128), 1) & 64) == 0
    sums = sums + jnp.where(
        first, jnp.roll(from_high[EDGE:], -64, 1), jnp.roll(from_low[EDGE:], 64, 1)
    )

    flat = sums.reshape(2, 8, 128).transpose(1, 0, 2).reshape(8, 256)
    from_low = shifted(jnp.concatenate([up_z, flat], axis=1), "gz", 1)
    from_high = shifted(jnp.concatenate([dn_z, flat], axis=1), "gz", -1)
    (acc,) = call(
        y_kernel,
        [grid],
        [VM] * 4,
        [(BANDS, CX, 32, 128)],
        "along_y",
        (same, y_low, y_high, acc),
        1 << 22,
        1 << 20,
    )
    (acc,) = call(
        whole_kernel,
        [grid],
        [HB, HB, HB] + [VM] * 3,
        [padded, (256, 128)] + PLACES + MATRICES + LISTED,
        "whole_blocks",
        (starts, owner_counts, matrices, projectors, sums, acc),
        1 << 30,
        1 << 24,
    )
    first = (iota((8, 256), 1) & 32) == 0
    flat = flat + jnp.where(
        first, jnp.roll(from_high[:, 512:], -32, 1), jnp.roll(from_low[:, 512:], 32, 1)
    )
    sums = flat.reshape(8, 2, 128).transpose(1, 0, 2).reshape(16, 128)
    (out,) = call(
        cut_kernel,
        [grid],
        [HB, HB, HB] + [VM] * 5,
        [padded, (256, 128)] + PLACES + MATRICES + LISTED,
        "cut_blocks",
        (
            starts,
            owner_counts,
            matrices,
            projectors,
            sums,
            from_low[:, :512],
            from_high[:, :512],
            acc,
        ),
        1 << 22,
        1 << 20,
    )
    return out


def solution(mesh):
    in_specs = (
        P(None, "gx", "gy", "gz"),
        P("gx", "gy", "gz"),
        P("gx", "gy", "gz", None, None, None, None),
        P("gx", "gy", "gz", None, None, None, None),
        P("gx", "gy", "gz", None, None, None),
        P("gx", "gy", "gz", None),
    )
    out_specs = P(None, "gx", "gy", "gz")
    return jax.shard_map(
        on_device, mesh=mesh, in_specs=in_specs, out_specs=out_specs, check_vma=False
    )
```

time: 61.9 us -> 59.5 us (0.961)
  the two profiles are of different devices: /device:TPU:6 before, /device:TPU:16 now
where the time goes in v2:
time: 59.5 us; the launch traced here: 59.2 us
  starting transfers between devices  31.1 us (52%)
  waiting for transfers between devices  16.1 us (27%)
  Pallas kernels  9.67 us (16%)
  local copies, waits for them, and re-layouts  1.85 us (3%)
    ppermute x6, starting transfers between devices, shifted(): lax.ppermute(value, axis, [(i, (i + distance) % n) for i in range(n)])  31.1 us
    ppermute x6, waiting for transfers between devices, shifted(): lax.ppermute(value, axis, [(i, (i + distance) % n) for i in range(n)])  16.1 us
    pallas_call x7, Pallas kernels, call(): pl.pallas_call(kernel, out_shape=outs, in_specs=ins, out_specs=[VM] * len...  9.67 us
    unnamed x12, local copies, waits for them, and re-layouts  1.52 us
  transfers between devices with their start and end apart: 6, of which 4 were waited for; matrix products, arithmetic and copies ran while one was open for 0% of the time, Pallas kernels for 6%

profile of v2, /device:TPU:16, one launch (start us, length us, event | category | flops | bytes accessed | tf_op | source)
XLA Modules:
  0.0 59.2 jit_solution(13316551462396991260)
XLA Ops:
  0.0 0.0 copy-start.3
  0.0 0.0 copy-start
  0.0 0.0 copy-start.4
  0.0 0.0 copy-start.5
  0.0 1.1 %copy-done.5 = f32[2,16,16,128]{3,2,1,0:T(8,128)S(1)} copy-done((f32[2,16,16,128]{3,2,1,0:T(8,128)S(1)}, f32[2,16,16,128]{3,2,1,0:T(8,128)}, u32[]{:S(2)}) %copy-start.5) | copy-done | bytes 262168
  1.1 0.2 turn.1
  1.3 0.0 copy-done.3
  1.3 0.4 copy-done
  1.7 0.0 copy-done.4
  1.7 0.0 copy-start.1
  1.7 2.8 %gather.1 = f32[16,128]{1,0:T(8,128)S(1)} custom-call(s32[1,1,1,3,4,8]{5,4,3,2,1,0:T(4,128)S(1)} %bitcast.35, s32[1,1,1,8]{3,2,1,0:T(1,128)S(1)} %copy-done.4, f32[2,17,48,128]{3,2,1,0:T(8,128)S(1)} %get-tuple-element.18.turned, f32[32,128,128]{2,1,0:T(8,128)S(1)} %bitcast.29), custom_call_target="tpu_custom_call" | custom-call | flops 1073741824 | bytes 16777216 | tf_op jit(solution)/shard_map/gather/pallas_call | solution.py:338
  4.5 0.0 copy-start.2
  4.6 17.4 %collective-permute-start = (f32[200,128]{1,0:T(8,128)S(1)}, f32[200,128]{1,0:T(8,128)S(1)}, u32[]{:S(2)}, u32[]{:S(2)}) collective-permute-start(f32[200,128]{1,0:T(8,128)S(1)} %pad_maximum_fusion.2), channel_id=1, source_target_pairs={{0,960},{64,0},{128,64},{192,128},{256,192},{320,256},{384,320},{4... | collective-permute-start | bytes 307208 | tf_op jit(solution)/shard_map/ppermute | solution.py:334
  22.0 1.9 %collective-permute-start.1 = (f32[200,128]{1,0:T(8,128)S(1)}, f32[200,128]{1,0:T(8,128)S(1)}, u32[]{:S(2)}, u32[]{:S(2)}) collective-permute-start(f32[200,128]{1,0:T(8,128)S(1)} %pad_maximum_fusion.3), channel_id=1, source_target_pairs={{0,64},{64,128},{128,192},{192,256},{256,320},{320,384},{384,448},... | collective-permute-start | bytes 307208 | tf_op jit(solution)/shard_map/ppermute | solution.py:334
  23.9 0.0 copy-done.1
  24.0 0.6 local.1
  24.5 0.0 collective-permute-done
  24.6 5.3 %collective-permute-done.1 = f32[200,128]{1,0:T(8,128)S(1)} collective-permute-done((f32[200,128]{1,0:T(8,128)S(1)}, f32[200,128]{1,0:T(8,128)S(1)}, u32[]{:S(2)}, u32[]{:S(2)}) %collective-permute-start.1) | collective-permute-done | bytes 102432 | tf_op jit(solution)/shard_map/ppermute | solution.py:334
  30.0 5.5 %collective-permute-start.3 = (f32[208,128]{1,0:T(8,128)S(1)}, f32[208,128]{1,0:T(8,128)S(1)}, u32[]{:S(2)}, u32[]{:S(2)}) collective-permute-start(f32[208,128]{1,0:T(8,128)S(1)} %get-tuple-element.37), channel_id=1, source_target_pairs={{0,16},{16,32},{32,48},{48,0},{1,17},{17,33},{33,49},{49,1},{2,18}... | collective-permute-start | bytes 319496 | tf_op jit(solution)/shard_map/ppermute | solution.py:334
  35.6 0.2 along_x.1.acc
  35.7 1.9 %collective-permute-start.2 = (f32[208,128]{1,0:T(8,128)S(1)}, f32[208,128]{1,0:T(8,128)S(1)}, u32[]{:S(2)}, u32[]{:S(2)}) collective-permute-start(f32[208,128]{1,0:T(8,128)S(1)} %get-tuple-element.38), channel_id=1, source_target_pairs={{0,48},{16,0},{32,16},{48,32},{1,49},{17,1},{33,17},{49,33},{2,50}... | collective-permute-start | bytes 319496 | tf_op jit(solution)/shard_map/ppermute | solution.py:334
  37.7 1.2 %collective-permute-done.3 = f32[208,128]{1,0:T(8,128)S(1)} collective-permute-done((f32[208,128]{1,0:T(8,128)S(1)}, f32[208,128]{1,0:T(8,128)S(1)}, u32[]{:S(2)}, u32[]{:S(2)}) %collective-permute-start.3) | collective-permute-done | bytes 106528 | tf_op jit(solution)/shard_map/ppermute | solution.py:334
  38.9 0.1 fusion.4
  38.9 7.8 %collective-permute-done.2 = f32[208,128]{1,0:T(8,128)S(1)} collective-permute-done((f32[208,128]{1,0:T(8,128)S(1)}, f32[208,128]{1,0:T(8,128)S(1)}, u32[]{:S(2)}, u32[]{:S(2)}) %collective-permute-start.2) | collective-permute-done | bytes 106528 | tf_op jit(solution)/shard_map/ppermute | solution.py:334
  46.7 0.1 fusion.5
  46.8 0.1 fusion.sums
  46.9 1.9 %collective-permute-start.4 = (f32[8,768]{1,0:T(8,128)S(1)}, f32[8,768]{1,0:T(8,128)S(1)}, u32[]{:S(2)}, u32[]{:S(2)}) collective-permute-start(f32[8,768]{1,0:T(8,128)S(1)} %get-tuple-element.36), channel_id=1, source_target_pairs={{0,15},{1,0},{2,1},{3,2},{4,3},{5,4},{6,5},{7,6},{8,7},{9,8},{10,9... | collective-permute-start | bytes 73736 | tf_op jit(solution)/shard_map/ppermute | solution.py:334
  48.8 2.4 %collective-permute-start.5 = (f32[8,768]{1,0:T(8,128)S(1)}, f32[8,768]{1,0:T(8,128)S(1)}, u32[]{:S(2)}, u32[]{:S(2)}) collective-permute-start(f32[8,768]{1,0:T(8,128)S(1)} %get-tuple-element.35), channel_id=1, source_target_pairs={{0,1},{1,2},{2,3},{3,4},{4,5},{5,6},{6,7},{7,8},{8,9},{9,10},{10,1... | collective-permute-start | bytes 73736 | tf_op jit(solution)/shard_map/ppermute | solution.py:334
  51.2 0.3 along_y.1.acc
  51.5 0.0 copy-done.2
  51.5 2.7 %whole_blocks.1.acc = f32[2,16,16,128]{3,2,1,0:T(8,128)S(1)} custom-call(s32[1,1,1,3,4,8]{5,4,3,2,1,0:T(4,128)S(1)} %bitcast.36, s32[1,1,1,8]{3,2,1,0:T(1,128)S(1)} %copy-done.4, f32[1,1,1,4,4,4,8]{6,5,4,3,2,1,0:T(4,128)S(1)} %bitcast.33, f32[32,128,128]{2,1,0:T(8,128)S(1)} %bitcast.30, f32[16,128]{1,0:T(8,128)S(1)} %fusion.sums, ...), custom_call_target="tpu_custom_call" | custom-call | flops 1073741824 | bytes 16777216 | tf_op jit(solution)/shard_map/whole_blocks/pallas_call | solution.py:338
  54.2 0.0 collective-permute-done.4
  54.2 0.1 slice.102
  54.3 1.7 %collective-permute-done.5 = f32[8,768]{1,0:T(8,128)S(1)} collective-permute-done((f32[8,768]{1,0:T(8,128)S(1)}, f32[8,768]{1,0:T(8,128)S(1)}, u32[]{:S(2)}, u32[]{:S(2)}) %collective-permute-start.5) | collective-permute-done | bytes 24608 | tf_op jit(solution)/shard_map/ppermute | solution.py:334
  56.0 0.1 slice.104
  56.1 0.1 fusion.3.sums
  56.2 3.0 %cut_blocks.1 = f32[2,16,16,128]{3,2,1,0:T(8,128)} custom-call(s32[1,1,1,3,4,8]{5,4,3,2,1,0:T(4,128)S(1)} %bitcast.37, s32[1,1,1,8]{3,2,1,0:T(1,128)S(1)} %copy-done.4, f32[1,1,1,4,4,4,8]{6,5,4,3,2,1,0:T(4,128)S(1)} %bitcast.34, f32[32,128,128]{2,1,0:T(8,128)S(1)} %bitcast.31, f32[16,128]{1,0:T(8,128)S(1)} %fusion.3.sums, f32[8,512]{1,0:T(8,128)S(1)} %slice.106.z_low, ...), custom_call_target="tpu_custom_call" | custom-call | flops 4194304 | bytes 1048576 | tf_op jit(solution)/shard_map/cut_blocks/pallas_call | solution.py:338
  (18 shorter events, 0.1 us)
Async XLA Ops:
  0.0 1.3 %copy-start.3 = (s32[1,1,1,8,4,3]{3,4,5,2,1,0:T(4,128)S(1)}, s32[1,1,1,8,4,3]{3,4,5,2,1,0:T(4,128)}, u32[]{:S(2)}) copy-start(s32[1,1,1,8,4,3]{3,4,5,2,1,0:T(4,128)} %param.10) | copy-start | bytes 1156
  0.0 1.7 %copy-start = (f32[1,1,1,8,4,4,4096]{6,5,4,3,2,1,0:T(4,128)S(1)}, f32[1,1,1,8,4,4,4096]{6,5,4,3,2,1,0:T(4,128)}, u32[]{:S(2)}) copy-start(f32[1,1,1,8,4,4,4096]{6,5,4,3,2,1,0:T(4,128)} %param.8) | copy-start | bytes 6291460
  0.0 1.7 %copy-start.4 = (s32[1,1,1,8]{3,2,1,0:T(1,128)S(1)}, s32[1,1,1,8]{3,2,1,0:T(1,128)}, u32[]{:S(2)}) copy-start(s32[1,1,1,8]{3,2,1,0:T(1,128)} %counts_in.5) | copy-start | bytes 100
  0.0 1.1 %copy-start.5 = (f32[2,16,16,128]{3,2,1,0:T(8,128)S(1)}, f32[2,16,16,128]{3,2,1,0:T(8,128)}, u32[]{:S(2)}) copy-start(f32[2,16,16,128]{3,2,1,0:T(8,128)} %x.1) | copy-start | bytes 786436
  1.7 22.3 %copy-start.1 = (f32[16,16,128]{2,1,0:T(8,128)S(1)}, f32[16,16,128]{2,1,0:T(8,128)}, u32[]{:S(2)}) copy-start(f32[16,16,128]{2,1,0:T(8,128)} %pot.1) | copy-start | bytes 393220
  4.5 47.0 %copy-start.2 = (f32[1,1,1,8,4,4,4]{3,6,5,4,2,1,0:T(4,128)S(1)}, f32[1,1,1,8,4,4,4]{3,6,5,4,2,1,0:T(4,128)}, u32[]{:S(2)}) copy-start(f32[1,1,1,8,4,4,4]{3,6,5,4,2,1,0:T(4,128)} %param.9) | copy-start | bytes 6148
  4.6 20.0 %collective-permute-start = (f32[200,128]{1,0:T(8,128)S(1)}, f32[200,128]{1,0:T(8,128)S(1)}, u32[]{:S(2)}, u32[]{:S(2)}) collective-permute-start(f32[200,128]{1,0:T(8,128)S(1)} %pad_maximum_fusion.2), channel_id=1, source_target_pairs={{0,960},{64,0},{128,64},{192,128},{256,192},{320,256},{384,320},{4... | collective-permute-start | bytes 307208 | tf_op jit(solution)/shard_map/ppermute | solution.py:334
  22.0 7.9 %collective-permute-start.1 = (f32[200,128]{1,0:T(8,128)S(1)}, f32[200,128]{1,0:T(8,128)S(1)}, u32[]{:S(2)}, u32[]{:S(2)}) collective-permute-start(f32[200,128]{1,0:T(8,128)S(1)} %pad_maximum_fusion.3), channel_id=1, source_target_pairs={{0,64},{64,128},{128,192},{192,256},{256,320},{320,384},{384,448},... | collective-permute-start | bytes 307208 | tf_op jit(solution)/shard_map/ppermute | solution.py:334
  30.0 8.9 %collective-permute-start.3 = (f32[208,128]{1,0:T(8,128)S(1)}, f32[208,128]{1,0:T(8,128)S(1)}, u32[]{:S(2)}, u32[]{:S(2)}) collective-permute-start(f32[208,128]{1,0:T(8,128)S(1)} %get-tuple-element.37), channel_id=1, source_target_pairs={{0,16},{16,32},{32,48},{48,0},{1,17},{17,33},{33,49},{49,1},{2,18}... | collective-permute-start | bytes 319496 | tf_op jit(solution)/shard_map/ppermute | solution.py:334
  35.7 11.0 %collective-permute-start.2 = (f32[208,128]{1,0:T(8,128)S(1)}, f32[208,128]{1,0:T(8,128)S(1)}, u32[]{:S(2)}, u32[]{:S(2)}) collective-permute-start(f32[208,128]{1,0:T(8,128)S(1)} %get-tuple-element.38), channel_id=1, source_target_pairs={{0,48},{16,0},{32,16},{48,32},{1,49},{17,1},{33,17},{49,33},{2,50}... | collective-permute-start | bytes 319496 | tf_op jit(solution)/shard_map/ppermute | solution.py:334
  46.9 7.4 %collective-permute-start.4 = (f32[8,768]{1,0:T(8,128)S(1)}, f32[8,768]{1,0:T(8,128)S(1)}, u32[]{:S(2)}, u32[]{:S(2)}) collective-permute-start(f32[8,768]{1,0:T(8,128)S(1)} %get-tuple-element.36), channel_id=1, source_target_pairs={{0,15},{1,0},{2,1},{3,2},{4,3},{5,4},{6,5},{7,6},{8,7},{9,8},{10,9... | collective-permute-start | bytes 73736 | tf_op jit(solution)/shard_map/ppermute | solution.py:334
  48.8 7.3 %collective-permute-start.5 = (f32[8,768]{1,0:T(8,128)S(1)}, f32[8,768]{1,0:T(8,128)S(1)}, u32[]{:S(2)}, u32[]{:S(2)}) collective-permute-start(f32[8,768]{1,0:T(8,128)S(1)} %get-tuple-element.35), channel_id=1, source_target_pairs={{0,1},{1,2},{2,3},{3,4},{4,5},{5,6},{6,7},{7,8},{8,9},{9,10},{10,1... | collective-permute-start | bytes 73736 | tf_op jit(solution)/shard_map/ppermute | solution.py:334

commit v3 on v2

--- a/solution.py
+++ b/solution.py
@@ -334,6 +334,12 @@
     return lax.ppermute(value, axis, [(i, (i + distance) % n) for i in range(n)])
 
 
+def swapped(value, axis, first):
+    n = lax.axis_size(axis)
+    pairs = [((first + i) % n, (first + (i ^ 1)) % n) for i in range(n)]
+    return lax.ppermute(value, axis, pairs)
+
+
 def call(kernel, outs, ins, scratch, name, args, flops, bytes_accessed):
     return pl.pallas_call(
         kernel,
@@ -407,8 +413,10 @@
     )
 
     flat = sums.reshape(2, 8, 128).transpose(1, 0, 2).reshape(8, 256)
-    from_low = shifted(jnp.concatenate([up_z, flat], axis=1), "gz", 1)
-    from_high = shifted(jnp.concatenate([dn_z, flat], axis=1), "gz", -1)
+    odd = lax.rem(lax.axis_index("gz"), 2) == 1
+    near = jnp.concatenate([jnp.where(odd, dn_z, up_z), flat], axis=1)
+    far = jnp.concatenate([jnp.where(odd, up_z, dn_z), flat], axis=1)
+    near = swapped(near, "gz", 0)
     (acc,) = call(
         y_kernel,
         [grid],
@@ -419,6 +427,10 @@
         1 << 22,
         1 << 20,
     )
+    far, acc = lax.optimization_barrier((far, acc))
+    far = swapped(far, "gz", 1)
+    from_high = jnp.where(odd, far, near)
+    from_low = jnp.where(odd, near, far)
     (acc,) = call(
         whole_kernel,
         [grid],

time: 59.5 us -> 59.6 us (level)
  the two profiles are of different devices: /device:TPU:16 before, /device:TPU:24 now
where the time goes in v3:
time: 59.6 us; the launch traced here: 59.7 us
  starting transfers between devices  33.4 us (56%)
  waiting for transfers between devices  12.6 us (21%)
  Pallas kernels  11.3 us (19%)
  local copies, waits for them, and re-layouts  1.85 us (3%)
    ppermute x4, starting transfers between devices, shifted(): lax.ppermute(value, axis, [(i, (i + distance) % n) for i in range(n)])  26.4 us
    ppermute x4, waiting for transfers between devices, shifted(): lax.ppermute(value, axis, [(i, (i + distance) % n) for i in range(n)])  12.6 us
    pallas_call x7, Pallas kernels, call(): pl.pallas_call(kernel, out_shape=outs, in_specs=ins, out_specs=[VM] * len...  11.3 us
    ppermute x2, starting transfers between devices, swapped(): return lax.ppermute(value, axis, pairs)  7.01 us
    unnamed x12, local copies, waits for them, and re-layouts  1.52 us
  transfers between devices with their start and end apart: 6, of which 3 were waited for; matrix products, arithmetic and copies ran while one was open for 0% of the time, Pallas kernels for 8%

profile of v3, /device:TPU:24, one launch (start us, length us, event | category | flops | bytes accessed | tf_op | source)
XLA Modules:
  0.0 59.7 jit_solution(16948669559748460844)
XLA Ops:
  0.0 0.0 copy-start.3
  0.0 0.0 copy-start
  0.0 0.0 copy-start.4
  0.0 0.0 copy-start.5
  0.0 1.1 %copy-done.5 = f32[2,16,16,128]{3,2,1,0:T(8,128)S(1)} copy-done((f32[2,16,16,128]{3,2,1,0:T(8,128)S(1)}, f32[2,16,16,128]{3,2,1,0:T(8,128)}, u32[]{:S(2)}) %copy-start.5) | copy-done | bytes 262168
  1.1 0.2 turn.1
  1.3 0.0 copy-done.3
  1.3 0.4 copy-done
  1.7 0.0 copy-done.4
  1.7 0.0 copy-start.1
  1.7 3.6 %gather.1 = f32[16,128]{1,0:T(8,128)S(1)} custom-call(s32[1,1,1,3,4,8]{5,4,3,2,1,0:T(4,128)S(1)} %bitcast.35, s32[1,1,1,8]{3,2,1,0:T(1,128)S(1)} %copy-done.4, f32[2,17,48,128]{3,2,1,0:T(8,128)S(1)} %get-tuple-element.20.turned, f32[32,128,128]{2,1,0:T(8,128)S(1)} %bitcast.29), custom_call_target="tpu_custom_call" | custom-call | flops 1073741824 | bytes 16777216 | tf_op jit(solution)/shard_map/gather/pallas_call | solution.py:344
  5.3 0.0 copy-start.2
  5.4 17.7 %collective-permute-start = (f32[200,128]{1,0:T(8,128)S(1)}, f32[200,128]{1,0:T(8,128)S(1)}, u32[]{:S(2)}, u32[]{:S(2)}) collective-permute-start(f32[200,128]{1,0:T(8,128)S(1)} %pad_maximum_fusion.2), channel_id=1, source_target_pairs={{0,960},{64,0},{128,64},{192,128},{256,192},{320,256},{384,320},{4... | collective-permute-start | bytes 307208 | tf_op jit(solution)/shard_map/ppermute | solution.py:334
  23.1 1.9 %collective-permute-start.1 = (f32[200,128]{1,0:T(8,128)S(1)}, f32[200,128]{1,0:T(8,128)S(1)}, u32[]{:S(2)}, u32[]{:S(2)}) collective-permute-start(f32[200,128]{1,0:T(8,128)S(1)} %pad_maximum_fusion.3), channel_id=1, source_target_pairs={{0,64},{64,128},{128,192},{192,256},{256,320},{320,384},{384,448},... | collective-permute-start | bytes 307208 | tf_op jit(solution)/shard_map/ppermute | solution.py:334
  25.1 0.0 copy-done.1
  25.1 0.6 local.1
  25.7 0.0 collective-permute-done
  25.7 5.2 %collective-permute-done.1 = f32[200,128]{1,0:T(8,128)S(1)} collective-permute-done((f32[200,128]{1,0:T(8,128)S(1)}, f32[200,128]{1,0:T(8,128)S(1)}, u32[]{:S(2)}, u32[]{:S(2)}) %collective-permute-start.1) | collective-permute-done | bytes 102432 | tf_op jit(solution)/shard_map/ppermute | solution.py:334
  30.9 4.8 %collective-permute-start.3 = (f32[208,128]{1,0:T(8,128)S(1)}, f32[208,128]{1,0:T(8,128)S(1)}, u32[]{:S(2)}, u32[]{:S(2)}) collective-permute-start(f32[208,128]{1,0:T(8,128)S(1)} %get-tuple-element.45), channel_id=1, source_target_pairs={{0,16},{16,32},{32,48},{48,0},{1,17},{17,33},{33,49},{49,1},{2,18}... | collective-permute-start | bytes 319496 | tf_op jit(solution)/shard_map/ppermute | solution.py:334
  35.7 1.9 %collective-permute-start.2 = (f32[208,128]{1,0:T(8,128)S(1)}, f32[208,128]{1,0:T(8,128)S(1)}, u32[]{:S(2)}, u32[]{:S(2)}) collective-permute-start(f32[208,128]{1,0:T(8,128)S(1)} %get-tuple-element.46), channel_id=1, source_target_pairs={{0,48},{16,0},{32,16},{48,32},{1,49},{17,1},{33,17},{49,33},{2,50}... | collective-permute-start | bytes 319496 | tf_op jit(solution)/shard_map/ppermute | solution.py:334
  37.7 0.2 along_x.1.acc
  37.9 1.9 %collective-permute-done.3 = f32[208,128]{1,0:T(8,128)S(1)} collective-permute-done((f32[208,128]{1,0:T(8,128)S(1)}, f32[208,128]{1,0:T(8,128)S(1)}, u32[]{:S(2)}, u32[]{:S(2)}) %collective-permute-start.3) | collective-permute-done | bytes 106528 | tf_op jit(solution)/shard_map/ppermute | solution.py:334
  39.8 5.5 %collective-permute-done.2 = f32[208,128]{1,0:T(8,128)S(1)} collective-permute-done((f32[208,128]{1,0:T(8,128)S(1)}, f32[208,128]{1,0:T(8,128)S(1)}, u32[]{:S(2)}, u32[]{:S(2)}) %collective-permute-start.2) | collective-permute-done | bytes 106528 | tf_op jit(solution)/shard_map/ppermute | solution.py:334
  45.3 0.3 along_y.1.acc
  45.6 0.1 fusion.4
  45.7 0.1 fusion.5
  45.8 0.1 fusion.sums
  45.8 1.9 %collective-permute-start.4 = (f32[8,768]{1,0:T(8,128)S(1)}, f32[8,768]{1,0:T(8,128)S(1)}, u32[]{:S(2)}, u32[]{:S(2)}) collective-permute-start(f32[8,768]{1,0:T(8,128)S(1)} %get-tuple-element.33), channel_id=1, source_target_pairs={{1,2},{2,1},{3,4},{4,3},{5,6},{6,5},{7,8},{8,7},{9,10},{10,9},{11,... | collective-permute-start | bytes 73736 | tf_op jit(solution)/shard_map/ppermute | solution.py:340
  47.8 5.1 %collective-permute-start.5 = (f32[8,768]{1,0:T(8,128)S(1)}, f32[8,768]{1,0:T(8,128)S(1)}, u32[]{:S(2)}, u32[]{:S(2)}) collective-permute-start(f32[8,768]{1,0:T(8,128)S(1)} %get-tuple-element.43), channel_id=1, source_target_pairs={{0,1},{1,0},{2,3},{3,2},{4,5},{5,4},{6,7},{7,6},{8,9},{9,8},{10,11... | collective-permute-start | bytes 73736 | tf_op jit(solution)/shard_map/ppermute | solution.py:340
  52.9 0.0 copy-done.2
  52.9 3.8 %whole_blocks.1.acc = f32[2,16,16,128]{3,2,1,0:T(8,128)S(1)} custom-call(s32[1,1,1,3,4,8]{5,4,3,2,1,0:T(4,128)S(1)} %bitcast.36, s32[1,1,1,8]{3,2,1,0:T(1,128)S(1)} %copy-done.4, f32[1,1,1,4,4,4,8]{6,5,4,3,2,1,0:T(4,128)S(1)} %bitcast.33, f32[32,128,128]{2,1,0:T(8,128)S(1)} %bitcast.30, f32[16,128]{1,0:T(8,128)S(1)} %fusion.sums, ...), custom_call_target="tpu_custom_call" | custom-call | flops 1073741824 | bytes 16777216 | tf_op jit(solution)/shard_map/whole_blocks/pallas_call | solution.py:344
  56.6 0.0 collective-permute-done.4
  56.7 0.0 collective-permute-done.5
  56.7 0.1 slice.104
  56.8 0.1 slice.106
  56.8 0.1 fusion.3.sums
  56.9 2.8 %cut_blocks.1 = f32[2,16,16,128]{3,2,1,0:T(8,128)} custom-call(s32[1,1,1,3,4,8]{5,4,3,2,1,0:T(4,128)S(1)} %bitcast.37, s32[1,1,1,8]{3,2,1,0:T(1,128)S(1)} %copy-done.4, f32[1,1,1,4,4,4,8]{6,5,4,3,2,1,0:T(4,128)S(1)} %bitcast.34, f32[32,128,128]{2,1,0:T(8,128)S(1)} %bitcast.31, f32[16,128]{1,0:T(8,128)S(1)} %fusion.3.sums, f32[8,512]{1,0:T(8,128)S(1)} %slice.108.z_low, ...), custom_call_target="tpu_custom_call" | custom-call | flops 4194304 | bytes 1048576 | tf_op jit(solution)/shard_map/cut_blocks/pallas_call | solution.py:344
  (20 shorter events, 0.1 us)
Async XLA Ops:
  0.0 1.3 %copy-start.3 = (s32[1,1,1,8,4,3]{3,4,5,2,1,0:T(4,128)S(1)}, s32[1,1,1,8,4,3]{3,4,5,2,1,0:T(4,128)}, u32[]{:S(2)}) copy-start(s32[1,1,1,8,4,3]{3,4,5,2,1,0:T(4,128)} %param.10) | copy-start | bytes 1156
  0.0 1.7 %copy-start = (f32[1,1,1,8,4,4,4096]{6,5,4,3,2,1,0:T(4,128)S(1)}, f32[1,1,1,8,4,4,4096]{6,5,4,3,2,1,0:T(4,128)}, u32[]{:S(2)}) copy-start(f32[1,1,1,8,4,4,4096]{6,5,4,3,2,1,0:T(4,128)} %param.8) | copy-start | bytes 6291460
  0.0 1.7 %copy-start.4 = (s32[1,1,1,8]{3,2,1,0:T(1,128)S(1)}, s32[1,1,1,8]{3,2,1,0:T(1,128)}, u32[]{:S(2)}) copy-start(s32[1,1,1,8]{3,2,1,0:T(1,128)} %counts_in.5) | copy-start | bytes 100
  0.0 1.1 %copy-start.5 = (f32[2,16,16,128]{3,2,1,0:T(8,128)S(1)}, f32[2,16,16,128]{3,2,1,0:T(8,128)}, u32[]{:S(2)}) copy-start(f32[2,16,16,128]{3,2,1,0:T(8,128)} %x.1) | copy-start | bytes 786436
  1.7 23.4 %copy-start.1 = (f32[16,16,128]{2,1,0:T(8,128)S(1)}, f32[16,16,128]{2,1,0:T(8,128)}, u32[]{:S(2)}) copy-start(f32[16,16,128]{2,1,0:T(8,128)} %pot.1) | copy-start | bytes 393220
  5.3 47.5 %copy-start.2 = (f32[1,1,1,8,4,4,4]{3,6,5,4,2,1,0:T(4,128)S(1)}, f32[1,1,1,8,4,4,4]{3,6,5,4,2,1,0:T(4,128)}, u32[]{:S(2)}) copy-start(f32[1,1,1,8,4,4,4]{3,6,5,4,2,1,0:T(4,128)} %param.9) | copy-start | bytes 6148
  5.4 20.3 %collective-permute-start = (f32[200,128]{1,0:T(8,128)S(1)}, f32[200,128]{1,0:T(8,128)S(1)}, u32[]{:S(2)}, u32[]{:S(2)}) collective-permute-start(f32[200,128]{1,0:T(8,128)S(1)} %pad_maximum_fusion.2), channel_id=1, source_target_pairs={{0,960},{64,0},{128,64},{192,128},{256,192},{320,256},{384,320},{4... | collective-permute-start | bytes 307208 | tf_op jit(solution)/shard_map/ppermute | solution.py:334
  23.1 7.8 %collective-permute-start.1 = (f32[200,128]{1,0:T(8,128)S(1)}, f32[200,128]{1,0:T(8,128)S(1)}, u32[]{:S(2)}, u32[]{:S(2)}) collective-permute-start(f32[200,128]{1,0:T(8,128)S(1)} %pad_maximum_fusion.3), channel_id=1, source_target_pairs={{0,64},{64,128},{128,192},{192,256},{256,320},{320,384},{384,448},... | collective-permute-start | bytes 307208 | tf_op jit(solution)/shard_map/ppermute | solution.py:334
  30.9 8.9 %collective-permute-start.3 = (f32[208,128]{1,0:T(8,128)S(1)}, f32[208,128]{1,0:T(8,128)S(1)}, u32[]{:S(2)}, u32[]{:S(2)}) collective-permute-start(f32[208,128]{1,0:T(8,128)S(1)} %get-tuple-element.45), channel_id=1, source_target_pairs={{0,16},{16,32},{32,48},{48,0},{1,17},{17,33},{33,49},{49,1},{2,18}... | collective-permute-start | bytes 319496 | tf_op jit(solution)/shard_map/ppermute | solution.py:334
  35.7 9.6 %collective-permute-start.2 = (f32[208,128]{1,0:T(8,128)S(1)}, f32[208,128]{1,0:T(8,128)S(1)}, u32[]{:S(2)}, u32[]{:S(2)}) collective-permute-start(f32[208,128]{1,0:T(8,128)S(1)} %get-tuple-element.46), channel_id=1, source_target_pairs={{0,48},{16,0},{32,16},{48,32},{1,49},{17,1},{33,17},{49,33},{2,50}... | collective-permute-start | bytes 319496 | tf_op jit(solution)/shard_map/ppermute | solution.py:334
  45.8 10.8 %collective-permute-start.4 = (f32[8,768]{1,0:T(8,128)S(1)}, f32[8,768]{1,0:T(8,128)S(1)}, u32[]{:S(2)}, u32[]{:S(2)}) collective-permute-start(f32[8,768]{1,0:T(8,128)S(1)} %get-tuple-element.33), channel_id=1, source_target_pairs={{1,2},{2,1},{3,4},{4,3},{5,6},{6,5},{7,8},{8,7},{9,10},{10,9},{11,... | collective-permute-start | bytes 73736 | tf_op jit(solution)/shard_map/ppermute | solution.py:340
  47.8 8.9 %collective-permute-start.5 = (f32[8,768]{1,0:T(8,128)S(1)}, f32[8,768]{1,0:T(8,128)S(1)}, u32[]{:S(2)}, u32[]{:S(2)}) collective-permute-start(f32[8,768]{1,0:T(8,128)S(1)} %get-tuple-element.43), channel_id=1, source_target_pairs={{0,1},{1,0},{2,3},{3,2},{4,5},{5,4},{6,7},{7,6},{8,9},{9,8},{10,11... | collective-permute-start | bytes 73736 | tf_op jit(solution)/shard_map/ppermute | solution.py:340
